TPU v7x, 256 devices: a whole 4x4x8 slice. The times are simulated.
256 devices in a mesh: space: 32 (over z, x), tm: 8 (over y, core).
Axes of the slice: x: 4, y: 4, z: 8, core: 2. Of those that a mesh axis runs over, the one named last changes fastest.
Arguments:
- frame_slab: float32 [65536, 4096], P('space', 'tm'), may hold values from -160 to 160
- pair_decay_rates: float32 [32], replicated, may hold values from -2 to 0.5
- pair_angular_frequencies: float32 [32], replicated, as said below
Outputs:
- spatial_modes: float32 [64, 65536], P(None, 'space')
- misfit_matrix: float32 [65536, 4096], P('space', 'tm')
- gradient: float32 [64], replicated
- gauss_newton: float32 [64, 64], replicated
Inputs may be any that keep to these rules, and one draw needn't show every extreme that they name: pair_angular_frequencies[k] lies within 0.5 of 2 pi (k + 1).
All inputs are finite; a program needn't handle non-finite values.
Results may differ from a plain program's by a relative error of at most 0.0003.
Values sent between devices are 32-bit elements; how exact they have to be, the bound alone decides.
No kernel may reach another device: no remote copies, remote signals or barrier semaphores. Data moves between devices by JAX's collectives and lax.ppermute only.
A program may use at most 64 MiB of HBM per device.

v0:
```python
import jax
import jax.numpy as jnp
from jax import lax
from jax.sharding import PartitionSpec as P

highest = lax.Precision.HIGHEST


def build_epoch_vectors(pair_decay_rates, pair_angular_frequencies, measured_epochs):
    shrinking_exponential = jnp.exp(pair_decay_rates[:, None] * measured_epochs[None, :])
    turning_radians = pair_angular_frequencies[:, None] * measured_epochs[None, :]
    joined_vectors = jnp.stack(
        [
            shrinking_exponential * jnp.cos(turning_radians),
            shrinking_exponential * jnp.sin(turning_radians),
        ],
        axis=1,
    )
    return joined_vectors.reshape(2 * pair_decay_rates.shape[0], measured_epochs.shape[0])


def coupling_table():
    return jnp.array([[[1.0, 0.0], [0.0, 1.0]], [[0.0, -1.0], [1.0, 0.0]]], dtype=jnp.float32)


def newton_terms(cross_term, mode_gram, slope_gram, magnitude_divisor):
    pairs = cross_term.shape[0] // 2
    coupling = coupling_table()
    cross_blocks = cross_term.reshape(pairs, 2, pairs, 2)
    indices = jnp.arange(pairs, dtype=jnp.int32)
    diagonal_blocks = cross_blocks[indices, :, indices, :]
    gradient = -magnitude_divisor * jnp.einsum(
        "puw,kuw->kp", coupling, diagonal_blocks, precision=highest
    )
    mode_blocks = mode_gram.reshape(pairs, 2, pairs, 2)
    slope_blocks = slope_gram.reshape(pairs, 2, pairs, 2)
    inner = jnp.einsum("kulv,kwlx->kuwlvx", mode_blocks, slope_blocks, precision=highest)
    gauss_newton = magnitude_divisor * jnp.einsum(
        "puw,kuwlvx,qvx->kplq", coupling, inner, coupling, precision=highest
    )
    return (gradient.reshape(2 * pairs), gauss_newton.reshape(2 * pairs, 2 * pairs))


def outer_sum(left, right):
    return jnp.dot(left, right.T, precision=highest, preferred_element_type=jnp.float32)


def local(frame_slab, pair_decay_rates, pair_angular_frequencies):
    point_count, epoch_number = frame_slab.shape
    epoch_partitions = lax.axis_size("tm")
    complete_epochs = epoch_number * epoch_partitions
    location_number = point_count * lax.axis_size("space")
    leading_shift = lax.axis_index("tm") * epoch_number
    every_instant = jnp.arange(complete_epochs, dtype=jnp.float32) / complete_epochs
    complete_basis = build_epoch_vectors(pair_decay_rates, pair_angular_frequencies, every_instant)
    complete_slope = complete_basis * every_instant[None, :]
    basis_gram = outer_sum(complete_basis, complete_basis)
    slope_gram = outer_sum(complete_slope, complete_slope)
    epoch_vector_set = lax.dynamic_slice_in_dim(complete_basis, leading_shift, epoch_number, 1)
    jacobian_lines = lax.dynamic_slice_in_dim(complete_slope, leading_shift, epoch_number, 1)
    projection_part = lax.dot_general(
        epoch_vector_set,
        frame_slab,
        (((1,), (1,)), ((), ())),
        precision=highest,
        preferred_element_type=jnp.float32,
    )
    factor = jnp.linalg.cholesky(basis_gram)
    projection = lax.psum(projection_part, "tm")
    spatial_modes = jax.scipy.linalg.cho_solve((factor, True), projection)
    fitted = lax.dot_general(
        spatial_modes,
        epoch_vector_set,
        (((0,), (0,)), ((), ())),
        precision=highest,
        preferred_element_type=jnp.float32,
    )
    misfit_matrix = frame_slab - fitted
    moment = lax.dot_general(
        misfit_matrix,
        jacobian_lines,
        (((1,), (1,)), ((), ())),
        precision=highest,
        preferred_element_type=jnp.float32,
    )
    cross_part = jnp.dot(
        spatial_modes, moment, precision=highest, preferred_element_type=jnp.float32
    )
    cross_term = lax.psum(cross_part, ("space", "tm"))
    mode_gram = lax.psum(outer_sum(spatial_modes, spatial_modes), "space")
    magnitude_divisor = 1.0 / (location_number * complete_epochs)
    gradient, gauss_newton = newton_terms(cross_term, mode_gram, slope_gram, magnitude_divisor)
    return (spatial_modes, misfit_matrix, gradient, gauss_newton)


def solution(mesh):
    placed = (P("space", "tm"), P(), P())
    return jax.shard_map(
        local,
        mesh=mesh,
        in_specs=placed,
        out_specs=(P(None, "space"), P("space", "tm"), P(), P()),
        check_vma=False,
    )
```

profile of v0, /device:TPU:1, one launch (start us, length us, event | category | flops | bytes accessed | tf_op | source)
XLA Modules:
  0.0 353.2 jit_solution(13412416265408002999)
XLA Ops:
  7.2 0.0 all-reduce.2.cloned.1.call-start
  7.2 2.6 fusion.6
  9.9 0.1 pad_maximum_fusion
  10.0 0.8 copy.37
  10.8 0.7 reshape.216
  11.5 7.0 %fusion.15 = f32[64,2048]{1,0:T(8,128)} fusion(f32[2048,512]{1,0:T(8,128)} %param.4, f32[64,4096]{1,0:T(8,128)S(1)} %reshape.216, s32[]{:T(128)S(6)} %select_n.11), kind=kOutput, calls=%fused_computation.26 | convolution fusion | flops 805306368 | bytes 4849668 | tf_op jit(solution)/shard_map/dot_general | solution.py:61
  18.6 0.0 all-reduce.2.cloned.1.call-update
  18.6 1.0 fusion.28
  19.6 0.1 copy.38
  19.6 5.8 %cholesky.16 = f32[64,64]{1,0:T(8,128)S(1)} custom-call(f32[64,64]{1,0:T(8,128)S(1)} %fusion.23), custom_call_target="Cholesky" | custom-call | tf_op jit(solution)/shard_map/jit(cholesky)/cholesky | solution.py:68
  25.5 0.6 compare_reduce_fusion
  26.2 0.7 fusion.18
  26.8 0.1 dynamic-slice
  26.9 4.9 %custom-call.10 = f32[1,64,64]{1,2,0:T(8,128)S(1)} custom-call(f32[1,64,64]{2,1,0:T(8,128)S(1)} %fusion.18), custom_call_target="InvertDiagBlocksLowerTriangular" | custom-call | tf_op jit(solution)/shard_map/jit(_cho_solve)/triangular_solve | solution.py:70
  31.8 2.7 convolution_bitcast_fusion.2
  34.6 52.0 %all-reduce.2.cloned.1.call-done = f32[64,2048]{1,0:T(8,128)} async-done(((f32[64,2048]{1,0:T(8,128)}), f32[64,2048]{1,0:T(8,128)}) %all-reduce.2.cloned.1.call-update) | async-done | bytes 524304 | tf_op jit(solution)/shard_map/psum | solution.py:69
  86.6 1.7 fusion.21
  88.3 0.8 fusion.19
  89.0 0.0 copy-start
  89.1 0.6 fusion.30
  89.6 6.6 %convolution_subtract_fusion = f32[2048,512]{1,0:T(8,128)} fusion(f32[2048,512]{1,0:T(8,128)} %param.4, f32[64,2048]{1,0:T(8,128)S(1)} %fusion.19, f32[64,4096]{1,0:T(8,128)S(1)} %reshape.216, s32[]{:T(128)S(6)} %select_n.11), kind=kOutput, calls=%fused_computation.1 | convolution fusion | flops 806354944 | bytes 9043972 | tf_op jit(solution)/shard_map/dot_general | solution.py:71
  96.2 0.0 copy-start.3
  96.3 0.0 copy-start.2
  96.3 1.1 reshape.219
  97.3 127.6 %psum.23 = f32[32,32,2,2]{3,1,2,0:T(8,128)} all-reduce(f32[32,32,2,2]{3,1,2,0:T(8,128)S(1)} %bitcast.63), channel_id=1, replica_groups=mesh['space'=32,'tm'=8] {'space'}, use_global_device_ids=true, to_apply=%region_4.5 | all-reduce | flops 4096 | bytes 32768 | tf_op jit(solution)/shard_map/psum | solution.py:90
  224.9 1.7 copy.42
  226.6 0.0 copy-done.3
  226.6 0.8 convolution_bitcast_fusion
  227.5 0.0 copy-done.2
  227.5 0.5 fusion.1
  228.0 0.5 copy.45
  228.4 1.3 reshape.221
  229.7 6.3 %fusion.10 = f32[2048,64]{0,1:T(8,128)S(1)} fusion(f32[2048,512]{1,0:T(8,128)} %convolution_subtract_fusion, f32[64,4096]{1,0:T(8,128)S(1)} %reshape.216, s32[]{:T(128)S(6)} %select_n.11, f32[512]{0:T(512)S(1)} %dynamic-slice), kind=kOutput, calls=%fused_computation.21 | convolution fusion | flops 805339136 | bytes 4851716 | tf_op jit(solution)/shard_map/dot_general | solution.py:79
  236.0 0.0 copy-done
  236.0 0.0 copy-start.1
  236.0 0.6 fusion.29
  236.6 1.1 reshape.217
  237.7 0.8 copy.39
  238.5 106.3 %psum.22 = f32[32,2,32,2]{3,1,2,0:T(2,128)S(1)} all-reduce(f32[32,2,32,2]{3,1,2,0:T(2,128)S(1)} %copy.39), channel_id=1, replica_groups=mesh['space'=32,'tm'=8] {'space','tm'}, use_global_device_ids=true, to_apply=%region_3.4 | all-reduce | flops 4096 | bytes 32768 | tf_op jit(solution)/shard_map/psum | solution.py:89
  344.8 0.7 gather_fusion
  345.5 0.0 copy-done.1
  345.5 0.1 fusion.2
  345.6 0.1 copy.41
  345.7 0.6 reshape.218
  (5 shorter events, 0.1 us)
Async XLA Ops:
  7.2 79.4 %all-reduce.2.cloned.1.call-start = ((), (), s32[]{:S(2)}) async-start(), calls=%async_computation | async-start | bytes 1048576 | tf_op jit(solution)/shard_map/psum | solution.py:69
  89.0 147.0 %copy-start = (f32[64,2048]{1,0:T(8,128)}, f32[64,2048]{1,0:T(8,128)S(1)}, u32[]{:S(2)}) copy-start(f32[64,2048]{1,0:T(8,128)S(1)} %fusion.19) | copy-start | bytes 1572868
  96.2 130.4 %copy-start.3 = (f32[2,2,2,1,1,1]{2,0,1,5,4,3:T(2,128)S(1)}, f32[2,2,2,1,1,1]{2,0,1,5,4,3:T(2,128)}, u32[]{:S(2)}) copy-start(f32[2,2,2,1,1,1]{2,0,1,5,4,3:T(2,128)} %constant.85) | copy-start | bytes 100
  96.3 131.2 %copy-start.2 = (f32[2,2,2,1,1]{2,0,1,4,3:T(2,128)S(1)}, f32[2,2,2,1,1]{2,0,1,4,3:T(2,128)}, u32[]{:S(2)}) copy-start(f32[2,2,2,1,1]{2,0,1,4,3:T(2,128)} %constant.86) | copy-start | bytes 100
  236.0 109.5 %copy-start.1 = (f32[2,2,2]{2,0,1:T(2,128)S(1)}, f32[2,2,2]{2,0,1:T(2,128)}, u32[]{:S(2)}) copy-start(f32[2,2,2]{2,0,1:T(2,128)} %constant.71.clone) | copy-start | bytes 100
Sparse Core Ops, SparseCore 0:
  18.7 67.8 all-reduce.1
where the time goes:
time: 354 us; the launch traced here: 353 us
  blocking collectives  234 us (66%)
  waiting for transfers between devices  52.1 us (15%)
  matrix products  28.7 us (8%)
  other arithmetic  14.8 us (4%)
  between operations  14.2 us (4%)
  local copies, waits for them, and re-layouts  9.48 us (3%)
    psum x1, blocking collectives, local(): mode_gram = lax.psum(outer_sum(spatial_modes, spatial_modes), 'space')  128 us
    psum x1, blocking collectives, local(): cross_term = lax.psum(cross_part, ('space', 'tm'))  106 us
    psum x1, waiting for transfers between devices, local(): projection = lax.psum(projection_part, 'tm')  52 us
  transfers between devices with their start and end apart: 1, of which 1 were waited for; matrix products, arithmetic and copies ran while one was open for 5% of the time, Pallas kernels for 0%

commit v1 on v0

v1 whole, which is shorter than its diff:
```python
import jax
import jax.numpy as jnp
from jax import lax
from jax.experimental import pallas as pl
from jax.experimental.pallas import tpu as pltpu
from jax.sharding import PartitionSpec as P

f32 = jnp.float32
bf16 = jnp.bfloat16
highest = lax.Precision.HIGHEST
VMEM = pl.BlockSpec(memory_space=pltpu.VMEM)
ANY = pl.BlockSpec(memory_space=pl.ANY)
PARAMS = pltpu.CompilerParams(vmem_limit_bytes=40 * 1024 * 1024)


def dot(a, b, precision=None):
    return lax.dot_general(
        a, b, (((1,), (0,)), ((), ())), precision=precision, preferred_element_type=f32
    )


def dot_nt(a, b, precision=None):
    return lax.dot_general(
        a, b, (((1,), (1,)), ((), ())), precision=precision, preferred_element_type=f32
    )


def split(x):
    hi = x.astype(bf16)
    lo = (x - hi.astype(f32)).astype(bf16)
    return hi, lo


def sine_or_cosine(theta, is_cosine):
    q = jnp.floor(theta * 0.6366197723675814 + 0.5)
    r = theta - q * 1.5703125
    r = r - q * 4.837512969970703125e-4
    r = r - q * 7.5497899548918821691e-8
    s = r * r
    sine = r + r * s * (
        -0.16666666666 + s * (0.0083333293858894631756 + s * (-0.000198393348360966317347 + s * 2.7181216275479732e-6))
    )
    cosine = 1.0 + s * (
        -0.5 + s * (0.0416666641831398010253906 + s * (-0.001388833043165504932 + s * 2.4390448796277409e-5))
    )
    n = q.astype(jnp.int32) + jnp.where(is_cosine, 1, 0)
    value = jnp.where((n & 1) == 1, cosine, sine)
    return jnp.where((n & 2) == 2, -value, value)


def lane_parameters(values):
    n = values.shape[1]
    rows = lax.broadcasted_iota(jnp.int32, (n, 4 * n), 0)
    lanes = lax.broadcasted_iota(jnp.int32, (n, 4 * n), 1)
    eye = lax.broadcasted_iota(jnp.int32, (n, n), 0) == lax.broadcasted_iota(jnp.int32, (n, n), 1)
    column = jnp.sum(jnp.where(eye, values, 0.0), axis=1, keepdims=True)
    hit = (lanes % (2 * n)) // 2 == rows
    return jnp.sum(jnp.where(hit, column, 0.0), axis=0, keepdims=True)


def basis_and_slope(rates, freqs, first, count, complete):
    width = 4 * rates.shape[1]
    rate = lane_parameters(rates)
    freq = lane_parameters(freqs)
    lanes = lax.broadcasted_iota(jnp.int32, (count, width), 1)
    steps = lax.broadcasted_iota(jnp.int32, (count, width), 0) + first
    t = steps.astype(f32) / complete
    value = jnp.exp(rate * t) * sine_or_cosine(freq * t, lanes % 2 == 0)
    return jnp.where(lanes < width // 2, value, value * t)


def half_index(tm):
    return (tm + tm // 2) % 2


def load_half(d_ref, buf, sems, start, chunks):
    rows = buf.shape[0] // chunks
    copies = []
    for i in range(chunks):
        piece = pl.ds(i * rows, rows)
        copy = pltpu.make_async_copy(
            d_ref.at[pl.ds(pl.multiple_of(start + i * rows, rows), rows)], buf.at[piece], sems.at[i]
        )
        copy.start()
        copies.append(copy)
    return copies


def project(copies, buf, w, out_ref):
    chunks = len(copies)
    rows = buf.shape[0] // chunks
    width = out_ref.shape[1]
    for i, copy in enumerate(copies):
        copy.wait()
        piece = pl.ds(i * rows, rows)
        hi, lo = split(buf[piece, :])
        both = dot(hi, w) + dot(lo, w)
        out_ref[piece, :] = both[:, :width] + both[:, width:]


def first_kernel(complete, d_ref, rates_ref, freqs_ref, out_ref, w_ref, buf, sems):
    tm = lax.axis_index("tm")
    half = buf.shape[0]
    copies = load_half(d_ref, buf, sems, (1 - half_index(tm)) * half, sems.shape[0])
    count = d_ref.shape[1]
    x = basis_and_slope(rates_ref[...], freqs_ref[...], tm * count, count, complete)
    hi, lo = split(x)
    width = x.shape[1]
    w_ref[:, :width] = hi
    w_ref[:, width:] = lo
    project(copies, buf, w_ref[...], out_ref)


def second_kernel(d_ref, w_ref, out_ref, buf, sems):
    tm = lax.axis_index("tm")
    half = buf.shape[0]
    copies = load_half(d_ref, buf, sems, half_index(tm) * half, sems.shape[0])
    project(copies, buf, w_ref[...], out_ref)


def swap_rows(x):
    rows = lax.broadcasted_iota(jnp.int32, x.shape, 0)
    n = x.shape[0]
    return jnp.where(rows % 2 == 0, pltpu.roll(x, n - 1, 0), pltpu.roll(x, 1, 0))


def swap_lanes(x):
    lanes = lax.broadcasted_iota(jnp.int32, x.shape, 1)
    n = x.shape[1]
    return jnp.where(lanes % 2 == 0, pltpu.roll(x, n - 1, 1), pltpu.roll(x, 1, 1))


def inverse(a):
    n = a.shape[0]
    rows = lax.broadcasted_iota(jnp.int32, (n, n), 0)
    lanes = lax.broadcasted_iota(jnp.int32, (n, n), 1)
    for j in range(n):
        pivot_row = a[j : j + 1, :]
        column = a[:, j : j + 1]
        scale = 1.0 / a[j : j + 1, j : j + 1]
        scaled = jnp.where(lanes[:1] == j, scale, pivot_row * scale)
        rest = jnp.where(lanes == j, 0.0, a) - column * scaled
        a = jnp.where(rows == j, scaled, rest)
    return a


def gram_kernel(complete, rates_ref, freqs_ref, after_ref, inverse_ref, slope_ref, basis_slope_ref, x_ref):
    del after_ref
    width = 4 * rates_ref.shape[1]
    half = width // 2
    x_ref[...] = basis_and_slope(rates_ref[...], freqs_ref[...], 0, complete, complete)
    total = jnp.zeros((width, width), f32)
    block = 1024
    for i in range(complete // block):
        x = x_ref[pl.ds(i * block, block), :]
        total = total + lax.dot_general(
            x, x, (((0,), (0,)), ((), ())), precision=highest, preferred_element_type=f32
        )
    gram = total[:half, :half]
    inv = inverse(gram)
    inverse_ref[...] = jnp.concatenate(
        [jnp.concatenate([inv, jnp.zeros_like(inv)], axis=1), jnp.zeros((half, width), f32)], axis=0
    )
    slope = pltpu.roll(total[half:, :], half, 1)
    lanes = lax.broadcasted_iota(jnp.int32, slope.shape, 1)
    rows = lax.broadcasted_iota(jnp.int32, slope.shape, 0)
    row_sign = jnp.where(rows % 2 == 0, -1.0, 1.0)
    lane_sign = jnp.where(lanes % 2 == 0, -1.0, 1.0)
    turned = row_sign * swap_rows(slope)
    slope_ref[0] = slope
    slope_ref[1] = lane_sign * swap_lanes(slope)
    slope_ref[2] = turned
    slope_ref[3] = lane_sign * swap_lanes(turned)
    basis_slope_ref[...] = pltpu.roll(total[:half, :], half, 1)


def modes_kernel(a_ref, b_ref, inverse_ref, modes_ref, message_ref):
    x = a_ref[...] + b_ref[...]
    width = x.shape[1]
    half = width // 2
    lanes = lax.broadcasted_iota(jnp.int32, x.shape, 1)
    x = jnp.where(lanes < half, dot(x, inverse_ref[...], highest), x)
    modes = jnp.transpose(x)[:half]
    modes_ref[...] = modes
    both = dot(modes, x, highest)
    rows = lax.broadcasted_iota(jnp.int32, both.shape, 0)
    lanes = lax.broadcasted_iota(jnp.int32, both.shape, 1)
    low = both[: half // 2]
    high = pltpu.roll(both[half // 2 :], half, 1)
    message_ref[: half // 2] = jnp.where(lanes[: half // 2] < half, low, high)
    column = lanes - half
    same = jnp.sum(jnp.where(rows == column, both, 0.0), axis=0, keepdims=True)
    swapped = jnp.where(column % 2 == 0, both, -both)
    partner = jnp.where(column % 2 == 0, column + 1, column - 1)
    turn = jnp.sum(jnp.where(rows == partner, swapped, 0.0), axis=0, keepdims=True)
    tail = lax.broadcasted_iota(jnp.int32, (8, width), 0)
    message_ref[half // 2 :] = jnp.where(tail == 0, same, jnp.where(tail == 1, turn, 0.0))


def misfit_kernel(d_ref, own_ref, other_ref, w_ref, modes_ref, misfit_ref, b_ref):
    tm = lax.axis_index("tm")
    step = pl.program_id(0)
    steps = pl.num_programs(0)
    half, width = own_ref.shape[0], 2 * own_ref.shape[0]

    @pl.when(step == 0)
    def _():
        top = jnp.transpose(w_ref[:, :width].astype(f32))[:half].astype(bf16)
        low = jnp.transpose(w_ref[:, width:].astype(f32))[:half].astype(bf16)
        b_ref[...] = jnp.concatenate([top, low, top, low], axis=0)

    rows = d_ref.shape[0]
    mine = (step // (steps // 2)) == half_index(tm)
    place = pl.ds(pl.multiple_of((step % (steps // 2)) * rows, rows), rows)
    modes = jnp.where(mine, own_ref[:, place], other_ref[:, place])
    modes_ref[...] = modes
    hi, lo = split(jnp.transpose(jnp.concatenate([modes, modes], axis=0)))
    fitted = dot(jnp.concatenate([hi, lo], axis=1), b_ref[...])
    misfit_ref[...] = d_ref[...] - fitted


def last_kernel(divisor, a_ref, b_ref, slope_ref, basis_slope_ref, gradient_ref, newton_ref):
    m = a_ref[...] + b_ref[...]
    width = m.shape[1]
    half = width // 2
    quarter = half // 2
    upper = m[:quarter]
    gram = jnp.concatenate([upper, pltpu.roll(upper, half, 1)], axis=0)
    rows = lax.broadcasted_iota(jnp.int32, gram.shape, 0)
    lanes = lax.broadcasted_iota(jnp.int32, gram.shape, 1)

    def block_sums(x):
        y = x + swap_rows(x)
        return y + swap_lanes(y)

    def for_row(first, second):
        return jnp.where(rows % 2 == 0, first, second)

    even = for_row(block_sums(gram * slope_ref[0]), block_sums(gram * slope_ref[2]))
    odd = for_row(block_sums(gram * slope_ref[1]), block_sums(gram * slope_ref[3]))
    newton = divisor * jnp.where(lanes % 2 == 0, even, odd)
    newton_ref[...] = newton[:, :half]
    basis_slope = basis_slope_ref[...]
    same = jnp.sum(gram * basis_slope, axis=0, keepdims=True)
    turn = jnp.sum(swap_lanes(gram) * basis_slope, axis=0, keepdims=True)
    tail = pltpu.roll(m[quarter:], half, 1)
    lane = lanes[:1]
    same = tail[0:1] - same
    turn = tail[1:2] - jnp.where(lane % 2 == 0, turn, -turn)
    same = same + swap_lanes(same)
    turn = turn + swap_lanes(turn)
    gradient_ref[...] = (-divisor * jnp.where(lane % 2 == 0, same, turn))[:, :half]


def flips(n, bits):
    return [(i, i ^ bits) for i in range(n)]


def local(frame_slab, pair_decay_rates, pair_angular_frequencies):
    points, epochs = frame_slab.shape
    pairs = pair_decay_rates.shape[0]
    basis = 2 * pairs
    width = 2 * basis
    tm_size, space_size = lax.axis_size("tm"), lax.axis_size("space")
    complete = epochs * tm_size
    half = points // 2
    divisor = 1.0 / (points * space_size * complete)
    rates = pair_decay_rates.reshape(1, pairs)
    freqs = pair_angular_frequencies.reshape(1, pairs)
    chunks = 4
    scratch = [pltpu.VMEM((half, epochs), f32), pltpu.SemaphoreType.DMA((chunks,))]

    away, w = pl.pallas_call(
        lambda *refs: first_kernel(complete, *refs),
        out_shape=(
            jax.ShapeDtypeStruct((half, width), f32),
            jax.ShapeDtypeStruct((epochs, 2 * width), bf16),
        ),
        in_specs=[ANY, VMEM, VMEM],
        out_specs=(VMEM, VMEM),
        scratch_shapes=scratch,
        compiler_params=PARAMS,
        name="project_away",
    )(frame_slab, rates, freqs)
    arrived = lax.ppermute(away, "tm", flips(tm_size, 1))
    kept = pl.pallas_call(
        second_kernel,
        out_shape=jax.ShapeDtypeStruct((half, width), f32),
        in_specs=[ANY, VMEM],
        out_specs=VMEM,
        scratch_shapes=scratch,
        compiler_params=PARAMS,
        cost_estimate=pl.CostEstimate(flops=2 * half * epochs * width * 4, bytes_accessed=half * epochs * 4, transcendentals=0),
        name="project_kept",
    )(frame_slab, w)
    inverse_gram, slopes, basis_slope = pl.pallas_call(
        lambda *refs: gram_kernel(complete, *refs),
        out_shape=(
            jax.ShapeDtypeStruct((width, width), f32),
            jax.ShapeDtypeStruct((4, basis, width), f32),
            jax.ShapeDtypeStruct((basis, width), f32),
        ),
        in_specs=[VMEM, VMEM, ANY],
        out_specs=(VMEM, VMEM, VMEM),
        scratch_shapes=[pltpu.VMEM((complete, width), f32)],
        compiler_params=PARAMS,
        cost_estimate=pl.CostEstimate(flops=10**9, bytes_accessed=10**7, transcendentals=10**6),
        name="grams",
    )(rates, freqs, kept)

    summed = kept + arrived
    quarter = half // 2
    first, second = summed[:quarter], summed[quarter:]
    near, wrap = flips(tm_size, 3), flips(tm_size, 7)
    first_in = lax.ppermute(first, "tm", near)
    second_in = lax.ppermute(second, "tm", wrap)
    first = first + first_in
    second = second + second_in
    first_in = lax.ppermute(first, "tm", wrap)
    second_in = lax.ppermute(second, "tm", near)
    modes_half, message = pl.pallas_call(
        modes_kernel,
        out_shape=(
            jax.ShapeDtypeStruct((basis, half), f32),
            jax.ShapeDtypeStruct((pairs + 8, width), f32),
        ),
        in_specs=[VMEM] * 3,
        out_specs=(VMEM, VMEM),
        compiler_params=PARAMS,
        name="modes",
    )(jnp.concatenate([first, second]), jnp.concatenate([first_in, second_in]), inverse_gram)

    message = message + lax.ppermute(message, "tm", flips(tm_size, 1))
    modes_other = lax.ppermute(modes_half, "tm", flips(tm_size, 1))
    block = 256
    steps = points // block
    spatial_modes, misfit = pl.pallas_call(
        misfit_kernel,
        grid=(steps,),
        out_shape=(
            jax.ShapeDtypeStruct((basis, points), f32),
            jax.ShapeDtypeStruct((points, epochs), f32),
        ),
        in_specs=[pl.BlockSpec((block, epochs), lambda i: (i, 0)), VMEM, VMEM, VMEM],
        out_specs=(
            pl.BlockSpec((basis, block), lambda i: (0, i)),
            pl.BlockSpec((block, epochs), lambda i: (i, 0)),
        ),
        scratch_shapes=[pltpu.VMEM((width * 2, epochs), bf16)],
        compiler_params=PARAMS,
        cost_estimate=pl.CostEstimate(flops=10**9, bytes_accessed=10**7, transcendentals=0),
        name="misfit",
    )(frame_slab, modes_half, modes_other, w)
    axes = ("space", "tm")
    total = space_size * tm_size
    incoming = None
    for bits in (1, 3, 4, 12, 28):
        if incoming is not None:
            message = message + incoming
        incoming = lax.ppermute(message, axes, flips(total, bits * tm_size + 1))
    gradient, gauss_newton = pl.pallas_call(
        lambda *refs: last_kernel(divisor, *refs),
        out_shape=(
            jax.ShapeDtypeStruct((1, basis), f32),
            jax.ShapeDtypeStruct((basis, basis), f32),
        ),
        in_specs=[VMEM] * 4,
        out_specs=(VMEM, VMEM),
        compiler_params=PARAMS,
        name="newton",
    )(message, incoming, slopes, basis_slope)
    return spatial_modes, misfit, gradient.reshape(basis), gauss_newton


def solution(mesh):
    return jax.shard_map(
        local,
        mesh=mesh,
        in_specs=(P("space", "tm"), P(), P()),
        out_specs=(P(None, "space"), P("space", "tm"), P(), P()),
        check_vma=False,
    )
```

time: 354 us -> 66.2 us (0.19)
  blocking collectives: 234 us -> 0 us
  waiting for transfers between devices: 52.1 us -> 16.9 us
  matrix products: 28.7 us -> 0 us
  starting transfers between devices: 0.04 us -> 22.5 us
  Pallas kernels: 0 us -> 22.2 us
  other arithmetic: 14.8 us -> 0.21 us
  between operations: 14.2 us -> 0.75 us
  local copies, waits for them, and re-layouts: 9.48 us -> 3.54 us
    psum x2 -> x0, blocking collectives: 234 us -> none  [the longest x1 128 us: local(): mode_gram = lax.psum(outer_sum(spatial_modes, spatial_modes), 'space')]
    psum x1 -> x0, waiting for transfers between devices: 52 us -> none  [local(): projection = lax.psum(projection_part, 'tm')]
    dot_general x10 -> x0, matrix products: 26.3 us -> none  [the longest x1 7.05 us: local(): lax.dot_general(epoch_vector_set, frame_slab, (((1,), (1,)), ((), ())), p...]
    ppermute x0 -> x12, starting transfers between devices: none -> 22.5 us  [the longest x5 14.6 us: local(): incoming = lax.ppermute(message, axes, flips(total, bits * tm_size + 1))]
    pallas_call x0 -> x6, Pallas kernels: none -> 22.2 us  [the longest x1 10.8 us: local(): pl.pallas_call(lambda *refs: gram_kernel(complete, *refs), out_shape=(jax...]
    ppermute x0 -> x12, waiting for transfers between devices: none -> 16.9 us  [the longest x5 8.29 us: local(): incoming = lax.ppermute(message, axes, flips(total, bits * tm_size + 1))]
    another operation x6 -> x0, other arithmetic: 12.1 us -> none  [the longest x3 6.52 us: local(): factor = jnp.linalg.cholesky(basis_gram)]
    reshape x6 -> x0, local copies, waits for them, and re-layouts: 5.59 us -> none  [the longest x2 1.91 us: newton_terms(): cross_blocks = cross_term.reshape(pairs, 2, pairs, 2)]
  transfers between devices with their start and end apart: 1 -> 12, of which waited for: 1 -> 8; matrix products, arithmetic and copies ran while one was open for 5% -> 0% of each run, Pallas kernels for 0% -> 20%
where the time goes in v1:
time: 66.2 us; the launch traced here: 66.1 us
  starting transfers between devices  22.5 us (34%)
  Pallas kernels  22.2 us (34%)
  waiting for transfers between devices  16.9 us (26%)
  local copies, waits for them, and re-layouts  3.54 us (5%)
  between operations  0.75 us (1%)
    ppermute x5, starting transfers between devices, local(): incoming = lax.ppermute(message, axes, flips(total, bits * tm_size + 1))  14.6 us
    pallas_call x1, Pallas kernels, local(): pl.pallas_call(lambda *refs: gram_kernel(complete, *refs), out_shape=(jax...  10.8 us
    ppermute x5, waiting for transfers between devices, local(): incoming = lax.ppermute(message, axes, flips(total, bits * tm_size + 1))  8.29 us
    ppermute x1, waiting for transfers between devices, local(): first_in = lax.ppermute(first, 'tm', near)  6.51 us
    pallas_call x1, Pallas kernels, local(): pl.pallas_call(misfit_kernel, grid=(steps,), out_shape=(jax.ShapeDtypeStr...  4.78 us
    unnamed x8, local copies, waits for them, and re-layouts  3.5 us
    ppermute x1, starting transfers between devices, local(): arrived = lax.ppermute(away, 'tm', flips(tm_size, 1))  3.33 us
    pallas_call x1, Pallas kernels, local(): pl.pallas_call(lambda *refs: first_kernel(complete, *refs), out_shape=(ja...  2.62 us
  transfers between devices with their start and end apart: 12, of which 8 were waited for; matrix products, arithmetic and copies ran while one was open for 0% of the time, Pallas kernels for 20%

profile of v1, /device:TPU:1, one launch (start us, length us, event | category | flops | bytes accessed | tf_op | source)
XLA Modules:
  0.0 66.1 jit_solution(14997147725404556251)
XLA Ops:
  0.6 0.0 copy-start
  0.6 2.2 %copy-done = f32[2048,512]{1,0:T(8,128)S(1)} copy-done((f32[2048,512]{1,0:T(8,128)S(1)}, f32[2048,512]{1,0:T(8,128)}, u32[]{:S(2)}) %copy-start) | copy-done | bytes 4194328
  2.8 0.0 copy-start.2
  2.8 0.7 copy-done.2
  3.5 0.0 copy-start.3
  3.5 0.7 copy-done.3
  4.1 2.6 %project_away.1 = (f32[1024,128]{1,0:T(8,128)S(1)}, bf16[512,256]{1,0:T(8,128)(2,1)S(1)}) custom-call(f32[2048,512]{1,0:T(8,128)S(1)} %copy-done, f32[1,32]{1,0:T(1,128)S(1)} %bitcast.3, f32[1,32]{1,0:T(1,128)S(1)} %bitcast.5), custom_call_target="tpu_custom_call" | custom-call | tf_op jit(solution)/shard_map/project_away/pallas_call | solution.py:273
  6.8 3.3 %collective-permute-start = (f32[1024,128]{1,0:T(8,128)S(1)}, f32[1024,128]{1,0:T(8,128)S(1)}, u32[]{:S(2)}, u32[]{:S(2)}) collective-permute-start(f32[1024,128]{1,0:T(8,128)S(1)} %get-tuple-element.16), channel_id=1, source_target_pairs={{0,1},{1,0},{2,3},{3,2},{4,5},{5,4},{6,7},{7,6},{8,9},{9,8},{10,11... | collective-permute-start | bytes 1572872 | tf_op jit(solution)/shard_map/ppermute | solution.py:285
  10.1 1.9 %project_kept.1.refs_2_ = f32[1024,128]{1,0:T(8,128)S(1)} custom-call(f32[2048,512]{1,0:T(8,128)S(1)} %copy-done, bf16[512,256]{1,0:T(8,128)(2,1)S(1)} %get-tuple-element.15.w_ref), custom_call_target="tpu_custom_call" | custom-call | flops 536870912 | bytes 2097152 | tf_op jit(solution)/shard_map/project_kept/pallas_call | solution.py:286
  12.0 0.0 collective-permute-done
  12.0 0.1 add.24
  12.1 0.1 collective-permute-start.1
  12.2 0.0 copy-start.1
  12.2 1.7 %collective-permute-start.2 = (f32[512,128]{1,0:T(8,128)S(1)}, f32[512,128]{1,0:T(8,128)S(1)}, u32[]{:S(2)}, u32[]{:S(2)}) collective-permute-start(f32[512,128]{1,0:T(8,128)S(1)} %get-tuple-element.29), channel_id=1, source_target_pairs={{0,7},{1,6},{2,5},{3,4},{4,3},{5,2},{6,1},{7,0},{8,15},{9,14},{10,... | collective-permute-start | bytes 786440 | tf_op jit(solution)/shard_map/ppermute | solution.py:316
  13.9 6.5 %collective-permute-done.1 = f32[512,128]{1,0:T(8,128)S(1)} collective-permute-done((f32[512,128]{1,0:T(8,128)S(1)}, f32[512,128]{1,0:T(8,128)S(1)}, u32[]{:S(2)}, u32[]{:S(2)}) %collective-permute-start.1) | collective-permute-done | bytes 262176 | tf_op jit(solution)/shard_map/ppermute | solution.py:315
  20.4 1.0 %collective-permute-done.2 = f32[512,128]{1,0:T(8,128)S(1)} collective-permute-done((f32[512,128]{1,0:T(8,128)S(1)}, f32[512,128]{1,0:T(8,128)S(1)}, u32[]{:S(2)}, u32[]{:S(2)}) %collective-permute-start.2) | collective-permute-done | bytes 262176 | tf_op jit(solution)/shard_map/ppermute | solution.py:316
  21.5 0.1 slice_add_fusion.1
  21.5 2.1 %collective-permute-start.3 = (f32[512,128]{1,0:T(8,128)S(1)}, f32[512,128]{1,0:T(8,128)S(1)}, u32[]{:S(2)}, u32[]{:S(2)}) collective-permute-start(f32[512,128]{1,0:T(8,128)S(1)} %get-tuple-element.26), channel_id=1, source_target_pairs={{0,7},{1,6},{2,5},{3,4},{4,3},{5,2},{6,1},{7,0},{8,15},{9,14},{10,... | collective-permute-start | bytes 786440 | tf_op jit(solution)/shard_map/ppermute | solution.py:319
  23.7 0.0 collective-permute-start.4
  23.7 10.8 %grams.1 = (f32[128,128]{1,0:T(8,128)S(1)}, f32[4,64,128]{2,1,0:T(8,128)S(1)}, f32[64,128]{1,0:T(8,128)S(1)}) custom-call(f32[1,32]{1,0:T(1,128)S(1)} %bitcast.4, f32[1,32]{1,0:T(1,128)S(1)} %bitcast.6, f32[1024,128]{1,0:T(8,128)S(1)} %project_kept.1.refs_2_), custom_call_target="tpu_custom_call" | custom-call | flops 1000000000 | bytes 10000000 | tf_op jit(solution)/shard_map/grams/pallas_call | solution.py:296
  34.5 0.0 collective-permute-done.3
  34.5 0.0 collective-permute-done.4
  34.6 1.3 %modes.1 = (f32[64,1024]{1,0:T(8,128)S(1)}, f32[40,128]{1,0:T(8,128)S(1)}) custom-call(f32[1024,128]{1,0:T(8,128)S(1)} %pad_maximum_fusion.a_ref, f32[1024,128]{1,0:T(8,128)S(1)} %pad_maximum_fusion.1.b_ref, f32[128,128]{1,0:T(8,128)S(1)} %get-tuple-element.17.inverse_ref), custom_call_target="tpu_custom_call" | custom-call | tf_op jit(solution)/shard_map/modes/pallas_call | solution.py:321
  35.9 0.2 collective-permute-start.5
  36.1 0.4 collective-permute-start.6
  36.4 1.1 %collective-permute-done.6 = f32[40,128]{1,0:T(8,128)S(1)} collective-permute-done((f32[40,128]{1,0:T(8,128)S(1)}, f32[40,128]{1,0:T(8,128)S(1)}, u32[]{:S(2)}, u32[]{:S(2)}) %collective-permute-start.6) | collective-permute-done | bytes 20512 | tf_op jit(solution)/shard_map/ppermute | solution.py:333
  37.5 1.3 %collective-permute-start.7 = (f32[40,128]{1,0:T(8,128)S(1)}, f32[40,128]{1,0:T(8,128)S(1)}, u32[]{:S(2)}, u32[]{:S(2)}) collective-permute-start(f32[40,128]{1,0:T(8,128)S(1)} %add.27), channel_id=1, source_target_pairs={{0,9},{1,8},{2,11},{3,10},{4,13},{5,12},{6,15},{7,14},{8,1},{9,0},... | collective-permute-start | bytes 61448 | tf_op jit(solution)/shard_map/ppermute | solution.py:360
  38.8 2.0 %collective-permute-done.7 = f32[40,128]{1,0:T(8,128)S(1)} collective-permute-done((f32[40,128]{1,0:T(8,128)S(1)}, f32[40,128]{1,0:T(8,128)S(1)}, u32[]{:S(2)}, u32[]{:S(2)}) %collective-permute-start.7) | collective-permute-done | bytes 20512 | tf_op jit(solution)/shard_map/ppermute | solution.py:360
  40.7 2.5 %collective-permute-start.8 = (f32[40,128]{1,0:T(8,128)S(1)}, f32[40,128]{1,0:T(8,128)S(1)}, u32[]{:S(2)}, u32[]{:S(2)}) collective-permute-start(f32[40,128]{1,0:T(8,128)S(1)} %add.28), channel_id=1, source_target_pairs={{0,25},{1,24},{2,27},{3,26},{4,29},{5,28},{6,31},{7,30},{8,17},{9,... | collective-permute-start | bytes 61448 | tf_op jit(solution)/shard_map/ppermute | solution.py:360
  43.2 1.9 %collective-permute-done.8 = f32[40,128]{1,0:T(8,128)S(1)} collective-permute-done((f32[40,128]{1,0:T(8,128)S(1)}, f32[40,128]{1,0:T(8,128)S(1)}, u32[]{:S(2)}, u32[]{:S(2)}) %collective-permute-start.8) | collective-permute-done | bytes 20512 | tf_op jit(solution)/shard_map/ppermute | solution.py:360
  45.1 1.7 %collective-permute-start.9 = (f32[40,128]{1,0:T(8,128)S(1)}, f32[40,128]{1,0:T(8,128)S(1)}, u32[]{:S(2)}, u32[]{:S(2)}) collective-permute-start(f32[40,128]{1,0:T(8,128)S(1)} %add.29), channel_id=1, source_target_pairs={{0,33},{1,32},{2,35},{3,34},{4,37},{5,36},{6,39},{7,38},{8,41},{9,... | collective-permute-start | bytes 61448 | tf_op jit(solution)/shard_map/ppermute | solution.py:360
  46.8 1.5 %collective-permute-done.9 = f32[40,128]{1,0:T(8,128)S(1)} collective-permute-done((f32[40,128]{1,0:T(8,128)S(1)}, f32[40,128]{1,0:T(8,128)S(1)}, u32[]{:S(2)}, u32[]{:S(2)}) %collective-permute-start.9) | collective-permute-done | bytes 20512 | tf_op jit(solution)/shard_map/ppermute | solution.py:360
  48.4 4.4 %collective-permute-start.10 = (f32[40,128]{1,0:T(8,128)S(1)}, f32[40,128]{1,0:T(8,128)S(1)}, u32[]{:S(2)}, u32[]{:S(2)}) collective-permute-start(f32[40,128]{1,0:T(8,128)S(1)} %add.30), channel_id=1, source_target_pairs={{0,97},{1,96},{2,99},{3,98},{4,101},{5,100},{6,103},{7,102},{8,105... | collective-permute-start | bytes 61448 | tf_op jit(solution)/shard_map/ppermute | solution.py:360
  52.7 1.5 %collective-permute-done.10 = f32[40,128]{1,0:T(8,128)S(1)} collective-permute-done((f32[40,128]{1,0:T(8,128)S(1)}, f32[40,128]{1,0:T(8,128)S(1)}, u32[]{:S(2)}, u32[]{:S(2)}) %collective-permute-start.10) | collective-permute-done | bytes 20512 | tf_op jit(solution)/shard_map/ppermute | solution.py:360
  54.2 4.8 %collective-permute-start.11 = (f32[40,128]{1,0:T(8,128)S(1)}, f32[40,128]{1,0:T(8,128)S(1)}, u32[]{:S(2)}, u32[]{:S(2)}) collective-permute-start(f32[40,128]{1,0:T(8,128)S(1)} %add.31.refs_0_), channel_id=1, source_target_pairs={{0,225},{1,224},{2,227},{3,226},{4,229},{5,228},{6,231},{7,230},{8... | collective-permute-start | bytes 61448 | tf_op jit(solution)/shard_map/ppermute | solution.py:360
  59.0 1.5 %collective-permute-done.11.refs_1_ = f32[40,128]{1,0:T(8,128)S(1)} collective-permute-done((f32[40,128]{1,0:T(8,128)S(1)}, f32[40,128]{1,0:T(8,128)S(1)}, u32[]{:S(2)}, u32[]{:S(2)}) %collective-permute-start.11) | collective-permute-done | bytes 20512 | tf_op jit(solution)/shard_map/ppermute | solution.py:360
  60.5 0.8 %newton.1 = (f32[1,64]{1,0:T(1,128)}, f32[64,64]{1,0:T(8,128)}) custom-call(f32[40,128]{1,0:T(8,128)S(1)} %add.31.refs_0_, f32[40,128]{1,0:T(8,128)S(1)} %collective-permute-done.11.refs_1_, f32[4,64,128]{2,1,0:T(8,128)S(1)} %get-tuple-element.22.refs_2_, f32[64,128]{1,0:T(8,128)S(1)} %get-tuple-element.23.refs_3_), custom_call_target="tpu_custom_call" | custom-call | tf_op jit(solution)/shard_map/newton/pallas_call | solution.py:361
  61.3 0.0 collective-permute-done.5.other_ref
  61.3 0.0 copy-done.1
  61.3 4.8 %misfit.1 = (f32[64,2048]{1,0:T(8,128)}, f32[2048,512]{1,0:T(8,128)}) custom-call(f32[2048,512]{1,0:T(8,128)S(1)} %copy-done.1, f32[64,1024]{1,0:T(8,128)S(1)} %get-tuple-element.18.own_ref, f32[64,1024]{1,0:T(8,128)S(1)} %collective-permute-done.5.other_ref, bf16[512,256]{1,0:T(8,128)(2,1)S(1)} %get-tuple-element.15.w_ref), custom_call_target="tpu_custom_call" | custom-call | flops 1000000000 | bytes 10000000 | tf_op jit(solution)/shard_map/misfit/pallas_call | solution.py:337
  (8 shorter events, 0.1 us)
Async XLA Ops:
  0.6 2.2 %copy-start = (f32[2048,512]{1,0:T(8,128)S(1)}, f32[2048,512]{1,0:T(8,128)}, u32[]{:S(2)}) copy-start(f32[2048,512]{1,0:T(8,128)} %d_ref.3) | copy-start | bytes 12582916
  2.8 0.7 copy-start.2
  3.5 0.7 copy-start.3
  6.8 5.2 %collective-permute-start = (f32[1024,128]{1,0:T(8,128)S(1)}, f32[1024,128]{1,0:T(8,128)S(1)}, u32[]{:S(2)}, u32[]{:S(2)}) collective-permute-start(f32[1024,128]{1,0:T(8,128)S(1)} %get-tuple-element.16), channel_id=1, source_target_pairs={{0,1},{1,0},{2,3},{3,2},{4,5},{5,4},{6,7},{7,6},{8,9},{9,8},{10,11... | collective-permute-start | bytes 1572872 | tf_op jit(solution)/shard_map/ppermute | solution.py:285
  12.1 8.3 %collective-permute-start.1 = (f32[512,128]{1,0:T(8,128)S(1)}, f32[512,128]{1,0:T(8,128)S(1)}, u32[]{:S(2)}, u32[]{:S(2)}) collective-permute-start(f32[512,128]{1,0:T(8,128)S(1)} %get-tuple-element.28), channel_id=1, source_target_pairs={{0,3},{1,2},{2,1},{3,0},{4,7},{5,6},{6,5},{7,4},{8,11},{9,10},{10,... | collective-permute-start | bytes 786440 | tf_op jit(solution)/shard_map/ppermute | solution.py:315
  12.2 49.1 %copy-start.1 = (f32[2048,512]{1,0:T(8,128)S(1)}, f32[2048,512]{1,0:T(8,128)}, u32[]{:S(2)}) copy-start(f32[2048,512]{1,0:T(8,128)} %d_ref.3) | copy-start | bytes 12582916
  12.2 9.3 %collective-permute-start.2 = (f32[512,128]{1,0:T(8,128)S(1)}, f32[512,128]{1,0:T(8,128)S(1)}, u32[]{:S(2)}, u32[]{:S(2)}) collective-permute-start(f32[512,128]{1,0:T(8,128)S(1)} %get-tuple-element.29), channel_id=1, source_target_pairs={{0,7},{1,6},{2,5},{3,4},{4,3},{5,2},{6,1},{7,0},{8,15},{9,14},{10,... | collective-permute-start | bytes 786440 | tf_op jit(solution)/shard_map/ppermute | solution.py:316
  21.5 13.0 %collective-permute-start.3 = (f32[512,128]{1,0:T(8,128)S(1)}, f32[512,128]{1,0:T(8,128)S(1)}, u32[]{:S(2)}, u32[]{:S(2)}) collective-permute-start(f32[512,128]{1,0:T(8,128)S(1)} %get-tuple-element.26), channel_id=1, source_target_pairs={{0,7},{1,6},{2,5},{3,4},{4,3},{5,2},{6,1},{7,0},{8,15},{9,14},{10,... | collective-permute-start | bytes 786440 | tf_op jit(solution)/shard_map/ppermute | solution.py:319
  23.7 10.9 %collective-permute-start.4 = (f32[512,128]{1,0:T(8,128)S(1)}, f32[512,128]{1,0:T(8,128)S(1)}, u32[]{:S(2)}, u32[]{:S(2)}) collective-permute-start(f32[512,128]{1,0:T(8,128)S(1)} %get-tuple-element.27), channel_id=1, source_target_pairs={{0,3},{1,2},{2,1},{3,0},{4,7},{5,6},{6,5},{7,4},{8,11},{9,10},{10,... | collective-permute-start | bytes 786440 | tf_op jit(solution)/shard_map/ppermute | solution.py:320
  35.9 25.4 %collective-permute-start.5 = (f32[64,1024]{1,0:T(8,128)S(1)}, f32[64,1024]{1,0:T(8,128)S(1)}, u32[]{:S(2)}, u32[]{:S(2)}) collective-permute-start(f32[64,1024]{1,0:T(8,128)S(1)} %get-tuple-element.18.own_ref), channel_id=1, source_target_pairs={{0,1},{1,0},{2,3},{3,2},{4,5},{5,4},{6,7},{7,6},{8,9},{9,8},{10,11... | collective-permute-start | bytes 786440 | tf_op jit(solution)/shard_map/ppermute | solution.py:334
  36.1 1.4 %collective-permute-start.6 = (f32[40,128]{1,0:T(8,128)S(1)}, f32[40,128]{1,0:T(8,128)S(1)}, u32[]{:S(2)}, u32[]{:S(2)}) collective-permute-start(f32[40,128]{1,0:T(8,128)S(1)} %get-tuple-element.21), channel_id=1, source_target_pairs={{0,1},{1,0},{2,3},{3,2},{4,5},{5,4},{6,7},{7,6},{8,9},{9,8},{10,11... | collective-permute-start | bytes 61448 | tf_op jit(solution)/shard_map/ppermute | solution.py:333
  37.5 3.2 %collective-permute-start.7 = (f32[40,128]{1,0:T(8,128)S(1)}, f32[40,128]{1,0:T(8,128)S(1)}, u32[]{:S(2)}, u32[]{:S(2)}) collective-permute-start(f32[40,128]{1,0:T(8,128)S(1)} %add.27), channel_id=1, source_target_pairs={{0,9},{1,8},{2,11},{3,10},{4,13},{5,12},{6,15},{7,14},{8,1},{9,0},... | collective-permute-start | bytes 61448 | tf_op jit(solution)/shard_map/ppermute | solution.py:360
  40.7 4.4 %collective-permute-start.8 = (f32[40,128]{1,0:T(8,128)S(1)}, f32[40,128]{1,0:T(8,128)S(1)}, u32[]{:S(2)}, u32[]{:S(2)}) collective-permute-start(f32[40,128]{1,0:T(8,128)S(1)} %add.28), channel_id=1, source_target_pairs={{0,25},{1,24},{2,27},{3,26},{4,29},{5,28},{6,31},{7,30},{8,17},{9,... | collective-permute-start | bytes 61448 | tf_op jit(solution)/shard_map/ppermute | solution.py:360
  45.1 3.2 %collective-permute-start.9 = (f32[40,128]{1,0:T(8,128)S(1)}, f32[40,128]{1,0:T(8,128)S(1)}, u32[]{:S(2)}, u32[]{:S(2)}) collective-permute-start(f32[40,128]{1,0:T(8,128)S(1)} %add.29), channel_id=1, source_target_pairs={{0,33},{1,32},{2,35},{3,34},{4,37},{5,36},{6,39},{7,38},{8,41},{9,... | collective-permute-start | bytes 61448 | tf_op jit(solution)/shard_map/ppermute | solution.py:360
  48.4 5.9 %collective-permute-start.10 = (f32[40,128]{1,0:T(8,128)S(1)}, f32[40,128]{1,0:T(8,128)S(1)}, u32[]{:S(2)}, u32[]{:S(2)}) collective-permute-start(f32[40,128]{1,0:T(8,128)S(1)} %add.30), channel_id=1, source_target_pairs={{0,97},{1,96},{2,99},{3,98},{4,101},{5,100},{6,103},{7,102},{8,105... | collective-permute-start | bytes 61448 | tf_op jit(solution)/shard_map/ppermute | solution.py:360
  54.2 6.2 %collective-permute-start.11 = (f32[40,128]{1,0:T(8,128)S(1)}, f32[40,128]{1,0:T(8,128)S(1)}, u32[]{:S(2)}, u32[]{:S(2)}) collective-permute-start(f32[40,128]{1,0:T(8,128)S(1)} %add.31.refs_0_), channel_id=1, source_target_pairs={{0,225},{1,224},{2,227},{3,226},{4,229},{5,228},{6,231},{7,230},{8... | collective-permute-start | bytes 61448 | tf_op jit(solution)/shard_map/ppermute | solution.py:360

commit v2 on v1

v2 whole, which is shorter than its diff:
```python
import jax
import jax.numpy as jnp
from jax import lax
from jax.experimental import pallas as pl
from jax.experimental.pallas import tpu as pltpu
from jax.sharding import PartitionSpec as P

f32 = jnp.float32
bf16 = jnp.bfloat16
highest = lax.Precision.HIGHEST
VMEM = pl.BlockSpec(memory_space=pltpu.VMEM)
HBM = pl.BlockSpec(memory_space=pltpu.HBM)
ANY = pl.BlockSpec(memory_space=pl.ANY)
PARAMS = pltpu.CompilerParams(vmem_limit_bytes=40 * 1024 * 1024)


def dot(a, b, precision=None):
    return lax.dot_general(
        a, b, (((1,), (0,)), ((), ())), precision=precision, preferred_element_type=f32
    )


def dot_nt(a, b, precision=None):
    return lax.dot_general(
        a, b, (((1,), (1,)), ((), ())), precision=precision, preferred_element_type=f32
    )


def split(x):
    hi = x.astype(bf16)
    lo = (x - hi.astype(f32)).astype(bf16)
    return hi, lo


def sine_or_cosine(theta, is_cosine):
    q = jnp.floor(theta * 0.6366197723675814 + 0.5)
    r = theta - q * 1.5703125
    r = r - q * 4.837512969970703125e-4
    r = r - q * 7.5497899548918821691e-8
    s = r * r
    sine = r + r * s * (
        -0.16666666666 + s * (0.0083333293858894631756 + s * (-0.000198393348360966317347 + s * 2.7181216275479732e-6))
    )
    cosine = 1.0 + s * (
        -0.5 + s * (0.0416666641831398010253906 + s * (-0.001388833043165504932 + s * 2.4390448796277409e-5))
    )
    n = q.astype(jnp.int32) + jnp.where(is_cosine, 1, 0)
    value = jnp.where((n & 1) == 1, cosine, sine)
    return jnp.where((n & 2) == 2, -value, value)


def lane_parameters(values):
    n = values.shape[1]
    rows = lax.broadcasted_iota(jnp.int32, (n, 4 * n), 0)
    lanes = lax.broadcasted_iota(jnp.int32, (n, 4 * n), 1)
    eye = lax.broadcasted_iota(jnp.int32, (n, n), 0) == lax.broadcasted_iota(jnp.int32, (n, n), 1)
    column = jnp.sum(jnp.where(eye, values, 0.0), axis=1, keepdims=True)
    hit = (lanes % (2 * n)) // 2 == rows
    return jnp.sum(jnp.where(hit, column, 0.0), axis=0, keepdims=True)


def decayed_waves(rates, freqs, t):
    lanes = lax.broadcasted_iota(jnp.int32, t.shape, 1)
    rate = lane_parameters(rates)
    freq = lane_parameters(freqs)
    return jnp.exp(rate * t) * sine_or_cosine(freq * t, lanes % 2 == 0)


def half_index(tm):
    return (tm + tm // 2) % 2


def load_half(d_hbm, buf, sems, side):
    half = buf.shape[0]
    rows = half // sems.shape[0]
    copies = []
    for i in range(sems.shape[0]):
        piece = pl.ds(pl.multiple_of(side * half + i * rows, rows), rows)
        copies.append(pltpu.make_async_copy(d_hbm.at[piece], buf.at[pl.ds(i * rows, rows)], sems.at[i]))
        copies[-1].start()
    return copies


def project(copies, buf, w, out_ref):
    width = out_ref.shape[1]
    half = width // 2
    count = out_ref.shape[0] // 2
    for copy in copies:
        copy.wait()

    def product(start):
        hi, lo = split(buf[start : start + count, :])
        both = dot(hi, w) + dot(lo, w)
        return both[:, :width] + both[:, width:]

    x, y = product(0), product(count)
    left = lax.broadcasted_iota(jnp.int32, x.shape, 1) < half
    out_ref[:count, :] = jnp.where(left, x, pltpu.roll(y, half, 1))
    out_ref[count:, :] = jnp.where(left, pltpu.roll(x, half, 1), y)


def first_kernel(complete, d_hbm, rates_hbm, freqs_hbm, out_ref, w_ref, rates_ref, freqs_ref, buf, sems, psems):
    tm = lax.axis_index("tm")
    rates_copy = pltpu.make_async_copy(rates_hbm, rates_ref, psems.at[0])
    freqs_copy = pltpu.make_async_copy(freqs_hbm, freqs_ref, psems.at[1])
    rates_copy.start()
    freqs_copy.start()
    copies = load_half(d_hbm, buf, sems, 1 - half_index(tm))
    rates_copy.wait()
    freqs_copy.wait()
    count, width = buf.shape[1], out_ref.shape[1]
    steps = lax.broadcasted_iota(jnp.int32, (count, width), 0) + tm * count
    lanes = lax.broadcasted_iota(jnp.int32, (count, width), 1)
    t = steps.astype(f32) / complete
    x = decayed_waves(rates_ref[...], freqs_ref[...], t)
    x = jnp.where(lanes < width // 2, x, x * t)
    hi, lo = split(x)
    w_ref[:, :width] = hi
    w_ref[:, width:] = lo
    project(copies, buf, w_ref[...], out_ref)


def second_kernel(d_hbm, w_ref, out_ref, buf, sems):
    copies = load_half(d_hbm, buf, sems, half_index(lax.axis_index("tm")))
    project(copies, buf, w_ref[...], out_ref)


def swap_rows(x):
    rows = lax.broadcasted_iota(jnp.int32, x.shape, 0)
    n = x.shape[0]
    return jnp.where(rows % 2 == 0, pltpu.roll(x, n - 1, 0), pltpu.roll(x, 1, 0))


def swap_lanes(x):
    lanes = lax.broadcasted_iota(jnp.int32, x.shape, 1)
    n = x.shape[1]
    return jnp.where(lanes % 2 == 0, pltpu.roll(x, n - 1, 1), pltpu.roll(x, 1, 1))


def inverse_2x2(x):
    scale = 1.0 / (x[0][0] * x[1][1] - x[0][1] * x[1][0])
    return [[x[1][1] * scale, -x[0][1] * scale], [-x[1][0] * scale, x[0][0] * scale]]


def product_2x2(x, y):
    return [[x[i][0] * y[0][j] + x[i][1] * y[1][j] for j in range(2)] for i in range(2)]


def difference_2x2(x, y):
    return [[x[i][j] - y[i][j] for j in range(2)] for i in range(2)]


def inverse_4x4(m):
    a, b = [row[:2] for row in m[:2]], [row[2:] for row in m[:2]]
    c, d = [row[:2] for row in m[2:]], [row[2:] for row in m[2:]]
    ai = inverse_2x2(a)
    aib, cai = product_2x2(ai, b), product_2x2(c, ai)
    si = inverse_2x2(difference_2x2(d, product_2x2(c, aib)))
    e01 = [[-v for v in row] for row in product_2x2(aib, si)]
    e10 = [[-v for v in row] for row in product_2x2(si, cai)]
    e00 = difference_2x2(ai, product_2x2(e01, cai))
    return [e00[0] + e01[0], e00[1] + e01[1], e10[0] + si[0], e10[1] + si[1]]


def inverse(a):
    n = a.shape[0]
    rows = lax.broadcasted_iota(jnp.int32, a.shape, 0)
    lanes = lax.broadcasted_iota(jnp.int32, a.shape, 1)
    lane = lanes[:1]
    for p in range(0, n, 4):
        columns = [jnp.broadcast_to(a[:, p + i : p + i + 1], a.shape) for i in range(4)]
        pivots = [a[p + i : p + i + 1, :] for i in range(4)]
        e = inverse_4x4([[columns[j][p + i : p + i + 1] for j in range(4)] for i in range(4)])
        new = []
        for i in range(4):
            row = (e[i][0] * pivots[0] + e[i][1] * pivots[1]) + (e[i][2] * pivots[2] + e[i][3] * pivots[3])
            for j in range(4):
                row = jnp.where(lane == p + j, e[i][j], row)
            new.append(row)
        taken = (columns[0] * new[0] + columns[1] * new[1]) + (columns[2] * new[2] + columns[3] * new[3])
        a = jnp.where((lanes >= p) & (lanes < p + 4), 0.0, a) - taken
        for i in range(4):
            a = jnp.where(rows == p + i, new[i], a)
    return a


def gram_kernel(complete, rates_ref, freqs_ref, after_ref, gram_ref, slope_ref, basis_slope_ref):
    del after_ref
    width = 4 * rates_ref.shape[1]
    half = width // 2
    rates, freqs = rates_ref[...], freqs_ref[...]
    total = jnp.zeros((2 * width, 2 * width), f32)
    block = 512
    rows = lax.broadcasted_iota(jnp.int32, (block, width), 0)
    lanes = lax.broadcasted_iota(jnp.int32, (block, width), 1)
    start = jnp.where(lanes < half, rows, rows + complete // 2)
    for i in range(complete // 2 // block):
        t = (start + i * block).astype(f32) / complete
        x = decayed_waves(rates, freqs, t)
        x = jnp.concatenate([x, x * t], axis=1)
        total = total + lax.dot_general(
            x, x, (((0,), (0,)), ((), ())), precision=highest, preferred_element_type=f32
        )

    def fold(i, j):
        block = total[i * width : (i + 1) * width, j * width : (j + 1) * width]
        return block[:half] + pltpu.roll(block[half:], half, 1)

    gram_ref[...] = fold(0, 0)
    basis_slope_ref[...] = fold(0, 1)
    slope = fold(1, 1)
    lanes = lax.broadcasted_iota(jnp.int32, slope.shape, 1)
    rows = lax.broadcasted_iota(jnp.int32, slope.shape, 0)
    row_sign = jnp.where(rows % 2 == 0, -1.0, 1.0)
    lane_sign = jnp.where(lanes % 2 == 0, -1.0, 1.0)
    turned = row_sign * swap_rows(slope)
    slope_ref[0] = slope
    slope_ref[1] = lane_sign * swap_lanes(slope)
    slope_ref[2] = turned
    slope_ref[3] = lane_sign * swap_lanes(turned)


def inverse_kernel(gram_ref, after_ref, inverse_ref):
    del after_ref
    half, width = gram_ref.shape
    inv = inverse(gram_ref[...])
    inv = jnp.where(lax.broadcasted_iota(jnp.int32, inv.shape, 1) < half, inv, 0.0)
    inverse_ref[:half] = inv
    inverse_ref[half:] = pltpu.roll(inv, half, 1)


def modes_kernel(first_ref, first_in_ref, second_ref, second_in_ref, product_ref, inverse_ref, modes_ref, message_ref):
    x = jnp.concatenate([first_ref[...] + first_in_ref[...], second_ref[...] + second_in_ref[...]], axis=0)
    x = dot(x, inverse_ref[...], highest)
    count, width = x.shape
    half, quarter = width // 2, width // 4
    flat = jnp.transpose(x)
    modes_ref[:, :count] = flat[:half]
    modes_ref[:, count:] = flat[half:]
    both = dot(flat, jnp.concatenate([x, product_ref[...]], axis=1), highest)
    gram = both[:half, :width] + pltpu.roll(both[half:, :width], half, 1)
    cross = both[:half, width:] + pltpu.roll(both[half:, width:], half, 1)
    rows = lax.broadcasted_iota(jnp.int32, cross.shape, 0)
    lanes = lax.broadcasted_iota(jnp.int32, cross.shape, 1)
    even = lanes % 2 == 0
    same = jnp.sum(jnp.where(rows == lanes, cross, 0.0), axis=0, keepdims=True)
    partner = jnp.where(even, lanes + 1, lanes - 1)
    turn = jnp.sum(jnp.where(rows == partner, jnp.where(even, cross, -cross), 0.0), axis=0, keepdims=True)
    sums = jnp.where(even[:1], same + swap_lanes(same), turn + swap_lanes(turn))
    eighth, group = quarter // 2, quarter // 4
    upper = jnp.where(lanes[:eighth] < half, gram[:eighth], pltpu.roll(gram[eighth:quarter], half, 1))
    lower = jnp.zeros((group, width), f32)
    for i in range(4):
        part = gram[quarter + i * group : quarter + (i + 1) * group]
        part = pltpu.roll(part, (i * quarter - quarter) % width, 1)
        lower = jnp.where(lanes[:group] // quarter == i, part, lower)
    packed = jnp.concatenate([upper, lower], axis=0)
    y = lax.axis_index("tm") // 2
    share = packed.shape[0] // 4
    part = packed[:share]
    for i in range(1, 4):
        part = jnp.where(y == i, packed[i * share : (i + 1) * share], part)
    message_ref[...] = jnp.concatenate([part, sums, jnp.zeros((8 - share - 1, width), f32)], axis=0)


def spread_kernel(a_ref, b_ref, after_ref, out_ref):
    del after_ref
    total = a_ref[...] + b_ref[...]
    for i in range(out_ref.shape[0]):
        out_ref[i] = total


def collect_kernel(messages_ref, after_ref, out_ref):
    del after_ref
    total = messages_ref[0]
    for i in range(1, messages_ref.shape[0]):
        total = total + messages_ref[i]
    y = lax.axis_index("tm") // 2
    n = total.shape[0]
    for i in range(out_ref.shape[0] // n):
        out_ref[i * n : (i + 1) * n] = jnp.where(y == i, total, 0.0)


def misfit_kernel(d_hbm, own_ref, other_ref, w_ref, modes_hbm, misfit_hbm, done_ref, out_ref, in_sems, sems, modes_sems):
    side = half_index(lax.axis_index("tm"))
    basis, half = own_ref.shape
    width = 2 * basis
    chunks = sems.shape[0]
    rows = 2 * half // chunks
    copies = []
    for i in range(chunks):
        piece = pl.ds(i * rows, rows)
        copies.append(pltpu.make_async_copy(d_hbm.at[piece], out_ref.at[piece], in_sems.at[i]))
        copies[-1].start()
    waits = []
    for i, (ref, place) in enumerate(((own_ref, side), (other_ref, 1 - side))):
        lanes = pl.ds(pl.multiple_of(place * half, half), half)
        copy = pltpu.make_async_copy(ref, modes_hbm.at[:, lanes], modes_sems.at[i])
        copy.start()
        waits.append(copy)
    top = jnp.transpose(w_ref[:, :width].astype(f32))[:basis].astype(bf16)
    low = jnp.transpose(w_ref[:, width:].astype(f32))[:basis].astype(bf16)
    b = jnp.concatenate([top, low, top, low], axis=0)
    for i in range(chunks):
        where, start = divmod(i * rows, half)
        modes = jnp.where(side == where, own_ref[:, start : start + rows], other_ref[:, start : start + rows])
        hi, lo = split(jnp.transpose(jnp.concatenate([modes, modes], axis=0)))
        piece = pl.ds(i * rows, rows)
        fitted = dot(jnp.concatenate([hi, lo], axis=1), b)
        copies[i].wait()
        out_ref[piece, :] = out_ref[piece, :] - fitted
        copy = pltpu.make_async_copy(out_ref.at[piece], misfit_hbm.at[piece], sems.at[i])
        copy.start()
        waits.append(copy)
    for copy in waits:
        copy.wait()
    done_ref[...] = jnp.zeros_like(done_ref)


def last_kernel(divisor, a_ref, b_ref, slope_ref, basis_slope_ref, gradient_ref, newton_ref):
    total = a_ref[...] + b_ref[...]
    width = total.shape[1]
    half, quarter, eighth = width // 2, width // 4, width // 8
    share = (eighth + eighth // 2) // 4
    packed = jnp.concatenate([total[i * 8 : i * 8 + share] for i in range(4)], axis=0)
    sums = total[share : share + 1]
    for i in range(1, 4):
        sums = sums + total[i * 8 + share : i * 8 + share + 1]
    upper, lower = packed[:eighth], packed[eighth:]
    parts = [upper, pltpu.roll(upper, half, 1)]
    for i in range(4):
        parts.append(pltpu.roll(lower, (quarter - i * quarter) % width, 1))
    wide = jnp.concatenate(parts + [jnp.zeros((half, width), f32)], axis=0)
    rows = lax.broadcasted_iota(jnp.int32, (half, width), 0)
    lanes = lax.broadcasted_iota(jnp.int32, (half, width), 1)
    gram = jnp.where(rows <= lanes, wide[:half], jnp.transpose(wide)[:half])

    def block_sums(x):
        y = x + swap_rows(x)
        return y + swap_lanes(y)

    def for_row(first, second):
        return jnp.where(rows % 2 == 0, first, second)

    even = for_row(block_sums(gram * slope_ref[0]), block_sums(gram * slope_ref[2]))
    odd = for_row(block_sums(gram * slope_ref[1]), block_sums(gram * slope_ref[3]))
    newton = divisor * jnp.where(lanes % 2 == 0, even, odd)
    newton_ref[...] = newton[:, :half]
    basis_slope = basis_slope_ref[...]
    lane = lanes[:1]
    same = jnp.sum(gram * basis_slope, axis=0, keepdims=True)
    turn = jnp.sum(swap_lanes(gram) * basis_slope, axis=0, keepdims=True)
    turn = jnp.where(lane % 2 == 0, turn, -turn)
    fitted = jnp.where(lane % 2 == 0, same + swap_lanes(same), turn + swap_lanes(turn))
    gradient_ref[...] = (-divisor * (sums - fitted))[:, :half]


def flips(n, bits):
    return [(i, i ^ bits) for i in range(n)]


def cost(flops, bytes_accessed):
    return pl.CostEstimate(flops=flops, bytes_accessed=bytes_accessed, transcendentals=0)


def local(frame_slab, pair_decay_rates, pair_angular_frequencies):
    points, epochs = frame_slab.shape
    pairs = pair_decay_rates.shape[0]
    basis = 2 * pairs
    width = 2 * basis
    tm_size, space_size = lax.axis_size("tm"), lax.axis_size("space")
    complete = epochs * tm_size
    half = points // 2
    quarter = half // 2
    divisor = 1.0 / (points * space_size * complete)
    in_hbm = lambda x: pltpu.with_memory_space_constraint(x, pltpu.HBM)
    rates = in_hbm(pair_decay_rates.reshape(1, pairs))
    freqs = in_hbm(pair_angular_frequencies.reshape(1, pairs))
    slab = in_hbm(frame_slab)
    scratch = [pltpu.VMEM((half, epochs), f32), pltpu.SemaphoreType.DMA((4,))]

    away, w, rates, freqs = pl.pallas_call(
        lambda *refs: first_kernel(complete, *refs),
        out_shape=(
            jax.ShapeDtypeStruct((half, width), f32),
            jax.ShapeDtypeStruct((epochs, 2 * width), bf16),
            jax.ShapeDtypeStruct((1, pairs), f32),
            jax.ShapeDtypeStruct((1, pairs), f32),
        ),
        in_specs=[HBM, HBM, HBM],
        out_specs=(VMEM,) * 4,
        scratch_shapes=scratch + [pltpu.SemaphoreType.DMA((2,))],
        compiler_params=PARAMS,
        name="project_away",
    )(slab, rates, freqs)
    arrived = lax.ppermute(away, "tm", flips(tm_size, 1))
    kept = pl.pallas_call(
        second_kernel,
        out_shape=jax.ShapeDtypeStruct((half, width), f32),
        in_specs=[HBM, VMEM],
        out_specs=VMEM,
        scratch_shapes=scratch,
        compiler_params=PARAMS,
        cost_estimate=cost(2 * half * epochs * width * 4, half * epochs * 4),
        name="project_kept",
    )(slab, w)

    near, wrap = flips(tm_size, 3), flips(tm_size, 7)
    summed = kept + arrived
    eighth = quarter // 2
    first, second, product = summed[:eighth], summed[eighth:quarter], summed[quarter:]
    first_in = lax.ppermute(first, "tm", near)
    second_in = lax.ppermute(second, "tm", wrap)
    gram, slopes, basis_slope = pl.pallas_call(
        lambda *refs: gram_kernel(complete, *refs),
        out_shape=(
            jax.ShapeDtypeStruct((basis, width), f32),
            jax.ShapeDtypeStruct((4, basis, width), f32),
            jax.ShapeDtypeStruct((basis, width), f32),
        ),
        in_specs=[VMEM, VMEM, ANY],
        out_specs=(VMEM, VMEM, VMEM),
        compiler_params=PARAMS,
        cost_estimate=cost(10**9, 10**7),
        name="grams",
    )(rates, freqs, kept)
    first, second, gram = lax.optimization_barrier((first + first_in, second + second_in, gram))
    first_in = lax.ppermute(first, "tm", wrap)
    second_in = lax.ppermute(second, "tm", near)
    inverse_gram = pl.pallas_call(
        inverse_kernel,
        out_shape=jax.ShapeDtypeStruct((width, width), f32),
        in_specs=[VMEM, ANY],
        out_specs=VMEM,
        compiler_params=PARAMS,
        cost_estimate=cost(10**9, 10**7),
        name="inverse",
    )(gram, first)
    modes_half, message = pl.pallas_call(
        modes_kernel,
        out_shape=(
            jax.ShapeDtypeStruct((basis, half), f32),
            jax.ShapeDtypeStruct((8, width), f32),
        ),
        in_specs=[VMEM] * 6,
        out_specs=(VMEM, VMEM),
        compiler_params=PARAMS,
        name="modes",
    )(first, first_in, second, second_in, product, inverse_gram)

    message_in = lax.ppermute(message, "tm", flips(tm_size, 1))
    modes_other = lax.ppermute(modes_half, "tm", flips(tm_size, 1))
    messages = pl.pallas_call(
        spread_kernel,
        out_shape=jax.ShapeDtypeStruct((space_size, *message.shape), f32),
        in_specs=[VMEM, VMEM, ANY],
        out_specs=VMEM,
        compiler_params=PARAMS,
        name="spread",
    )(message, message_in, modes_other)
    messages = lax.all_to_all(messages, "space", 0, 0)
    blocks = 8
    spatial_modes, misfit, done = pl.pallas_call(
        misfit_kernel,
        out_shape=(
            jax.ShapeDtypeStruct((basis, points), f32),
            jax.ShapeDtypeStruct((points, epochs), f32),
            jax.ShapeDtypeStruct((8, width), f32),
        ),
        in_specs=[HBM, VMEM, VMEM, VMEM],
        out_specs=(HBM, HBM, VMEM),
        scratch_shapes=[pltpu.VMEM((points, epochs), f32)] + [pltpu.SemaphoreType.DMA((n,)) for n in (blocks, blocks, 2)],
        compiler_params=PARAMS,
        cost_estimate=cost(10**9, 10**7),
        name="misfit",
    )(slab, modes_half, modes_other, w)
    total = pl.pallas_call(
        collect_kernel,
        out_shape=jax.ShapeDtypeStruct((32, width), f32),
        in_specs=[VMEM, ANY],
        out_specs=VMEM,
        compiler_params=PARAMS,
        name="collect",
    )(messages, done)
    total = total + lax.ppermute(total, "tm", near)
    total_in = lax.ppermute(total, "tm", wrap)
    gradient, gauss_newton = pl.pallas_call(
        lambda *refs: last_kernel(divisor, *refs),
        out_shape=(
            jax.ShapeDtypeStruct((1, basis), f32),
            jax.ShapeDtypeStruct((basis, basis), f32),
        ),
        in_specs=[VMEM] * 4,
        out_specs=(VMEM, VMEM),
        compiler_params=PARAMS,
        name="newton",
    )(total, total_in, slopes, basis_slope)
    return spatial_modes, misfit, gradient.reshape(basis), gauss_newton


def solution(mesh):
    return jax.shard_map(
        local,
        mesh=mesh,
        in_specs=(P("space", "tm"), P(), P()),
        out_specs=(P(None, "space"), P("space", "tm"), P(), P()),
        check_vma=False,
    )
```

time: 66.2 us -> 55.5 us (0.84)
  Pallas kernels: 22.2 us -> 18.6 us
  local copies, waits for them, and re-layouts: 3.54 us -> 0.04 us
  waiting for transfers between devices: 16.9 us -> 13.5 us
    all_to_all x0 -> x1, starting transfers between devices: none -> 10.6 us  [local(): messages = lax.all_to_all(messages, 'space', 0, 0)]
    ppermute x6 -> x3, starting transfers between devices: 15 us -> 4.95 us  [the longest x1 3.37 us: local(): total_in = lax.ppermute(total, 'tm', wrap)]
    pallas_call x1, Pallas kernels: 10.8 us -> 3.83 us  [local(): pl.pallas_call(lambda *refs: gram_kernel(complete, *refs), out_shape=(jax...]
    ppermute x1, waiting for transfers between devices: 6.51 us -> 0.25 us  [local(): first_in = lax.ppermute(first, 'tm', near)]
    all_to_all x0 -> x1, waiting for transfers between devices: none -> 5.06 us  [local(): messages = lax.all_to_all(messages, 'space', 0, 0)]
    ppermute x6 -> x3, waiting for transfers between devices: 9.35 us -> 4.49 us  [the longest x1 2.04 us: local(): total = total + lax.ppermute(total, 'tm', near)]
    unnamed x8 -> x0, local copies, waits for them, and re-layouts: 3.5 us -> none
    pallas_call x1 -> x4, Pallas kernels: 4.78 us -> 7.88 us  [the longest x1 4.28 us: local(): pl.pallas_call(misfit_kernel, out_shape=(jax.ShapeDtypeStruct((basis, poi...]
  transfers between devices with their start and end apart: 12 -> 10, of which waited for: 8 -> 8; matrix products, arithmetic and copies ran while one was open for 0% -> 0% of each run, Pallas kernels for 20% -> 24%
where the time goes in v2:
time: 55.5 us; the launch traced here: 55.3 us
  starting transfers between devices  22.4 us (40%)
  Pallas kernels  18.6 us (34%)
  waiting for transfers between devices  13.5 us (24%)
  between operations  0.72 us (1%)
    all_to_all x1, starting transfers between devices, local(): messages = lax.all_to_all(messages, 'space', 0, 0)  10.6 us
    all_to_all x1, waiting for transfers between devices, local(): messages = lax.all_to_all(messages, 'space', 0, 0)  5.06 us
    pallas_call x1, Pallas kernels, local(): pl.pallas_call(misfit_kernel, out_shape=(jax.ShapeDtypeStruct((basis, poi...  4.28 us
    pallas_call x1, Pallas kernels, local(): pl.pallas_call(lambda *refs: gram_kernel(complete, *refs), out_shape=(jax...  3.83 us
    ppermute x1, starting transfers between devices, local(): total_in = lax.ppermute(total, 'tm', wrap)  3.37 us
    ppermute x1, starting transfers between devices, local(): arrived = lax.ppermute(away, 'tm', flips(tm_size, 1))  3.33 us
    pallas_call x1, Pallas kernels, local(): pl.pallas_call(inverse_kernel, out_shape=jax.ShapeDtypeStruct((width, wid...  2.9 us
    pallas_call x1, Pallas kernels, local(): pl.pallas_call(lambda *refs: first_kernel(complete, *refs), out_shape=(ja...  2.39 us
  transfers between devices with their start and end apart: 10, of which 8 were waited for; matrix products, arithmetic and copies ran while one was open for 0% of the time, Pallas kernels for 24%

profile of v2, /device:TPU:1, one launch (start us, length us, event | category | flops | bytes accessed | tf_op | source)
XLA Modules:
  0.0 55.3 jit_solution(510686741342490095)
XLA Ops:
  0.6 2.4 %project_away.1 = (f32[1024,128]{1,0:T(8,128)S(1)}, bf16[512,256]{1,0:T(8,128)(2,1)S(1)}, f32[1,32]{1,0:T(1,128)S(1)}, f32[1,32]{1,0:T(1,128)S(1)}) custom-call(f32[2048,512]{1,0:T(8,128)} %d_hbm.3, f32[1,32]{1,0:T(1,128)} %bitcast.3, f32[1,32]{1,0:T(1,128)} %bitcast.4), custom_call_target="tpu_custom_call" | custom-call | tf_op jit(solution)/shard_map/project_away/pallas_call | solution.py:382
  3.0 3.3 %collective-permute-start = (f32[1024,128]{1,0:T(8,128)S(1)}, f32[1024,128]{1,0:T(8,128)S(1)}, u32[]{:S(2)}, u32[]{:S(2)}) collective-permute-start(f32[1024,128]{1,0:T(8,128)S(1)} %get-tuple-element.22), channel_id=1, source_target_pairs={{0,1},{1,0},{2,3},{3,2},{4,5},{5,4},{6,7},{7,6},{8,9},{9,8},{10,11... | collective-permute-start | bytes 1572872 | tf_op jit(solution)/shard_map/ppermute | solution.py:396
  6.4 2.4 %project_kept.1.refs_2_ = f32[1024,128]{1,0:T(8,128)S(1)} custom-call(f32[2048,512]{1,0:T(8,128)} %d_hbm.3, bf16[512,256]{1,0:T(8,128)(2,1)S(1)} %get-tuple-element.21.w_ref), custom_call_target="tpu_custom_call" | custom-call | flops 536870912 | bytes 2097152 | tf_op jit(solution)/shard_map/project_kept/pallas_call | solution.py:397
  8.7 0.0 collective-permute-done
  8.7 0.1 add.12
  8.8 1.0 %collective-permute-start.2 = (f32[256,128]{1,0:T(8,128)S(1)}, f32[256,128]{1,0:T(8,128)S(1)}, u32[]{:S(2)}, u32[]{:S(2)}) collective-permute-start(f32[256,128]{1,0:T(8,128)S(1)} %get-tuple-element.40), channel_id=1, source_target_pairs={{0,7},{1,6},{2,5},{3,4},{4,3},{5,2},{6,1},{7,0},{8,15},{9,14},{10,... | collective-permute-start | bytes 393224 | tf_op jit(solution)/shard_map/ppermute | solution.py:413
  9.8 0.2 collective-permute-start.1
  10.0 3.8 %grams.1 = (f32[64,128]{1,0:T(8,128)S(1)}, f32[4,64,128]{2,1,0:T(8,128)S(1)}, f32[64,128]{1,0:T(8,128)S(1)}) custom-call(f32[1,32]{1,0:T(1,128)S(1)} %get-tuple-element.23.refs_0_, f32[1,32]{1,0:T(1,128)S(1)} %get-tuple-element.24.refs_1_, f32[1024,128]{1,0:T(8,128)S(1)} %project_kept.1.refs_2_), custom_call_target="tpu_custom_call" | custom-call | flops 1000000000 | bytes 10000000 | tf_op jit(solution)/shard_map/grams/pallas_call | solution.py:414
  13.9 1.4 %collective-permute-done.2 = f32[256,128]{1,0:T(8,128)S(1)} collective-permute-done((f32[256,128]{1,0:T(8,128)S(1)}, f32[256,128]{1,0:T(8,128)S(1)}, u32[]{:S(2)}, u32[]{:S(2)}) %collective-permute-start.2) | collective-permute-done | bytes 131104 | tf_op jit(solution)/shard_map/ppermute | solution.py:413
  15.2 0.2 collective-permute-done.1
  15.5 2.1 %collective-permute-start.3 = (f32[256,128]{1,0:T(8,128)S(1)}, f32[256,128]{1,0:T(8,128)S(1)}, u32[]{:S(2)}, u32[]{:S(2)}) collective-permute-start(f32[256,128]{1,0:T(8,128)S(1)} %get-tuple-element.26.after_ref.first_ref), channel_id=1, source_target_pairs={{0,7},{1,6},{2,5},{3,4},{4,3},{5,2},{6,1},{7,0},{8,15},{9,14},{10,... | collective-permute-start | bytes 393224 | tf_op jit(solution)/shard_map/ppermute | solution.py:428
  17.6 0.0 collective-permute-start.4
  17.6 2.9 %inverse.1.inverse_ref = f32[128,128]{1,0:T(8,128)S(1)} custom-call(f32[64,128]{1,0:T(8,128)S(1)} %get-tuple-element.28.gram_ref, f32[256,128]{1,0:T(8,128)S(1)} %get-tuple-element.26.after_ref.first_ref), custom_call_target="tpu_custom_call" | custom-call | flops 1000000000 | bytes 10000000 | tf_op jit(solution)/shard_map/inverse/pallas_call | solution.py:430
  20.5 1.8 %collective-permute-done.3.first_in_ref = f32[256,128]{1,0:T(8,128)S(1)} collective-permute-done((f32[256,128]{1,0:T(8,128)S(1)}, f32[256,128]{1,0:T(8,128)S(1)}, u32[]{:S(2)}, u32[]{:S(2)}) %collective-permute-start.3) | collective-permute-done | bytes 131104 | tf_op jit(solution)/shard_map/ppermute | solution.py:428
  22.3 0.5 collective-permute-done.4.second_in_ref
  22.8 1.2 %modes.1 = (f32[64,1024]{1,0:T(8,128)S(1)}, f32[8,128]{1,0:T(8,128)S(1)}) custom-call(f32[256,128]{1,0:T(8,128)S(1)} %get-tuple-element.26.after_ref.first_ref, f32[256,128]{1,0:T(8,128)S(1)} %collective-permute-done.3.first_in_ref, f32[256,128]{1,0:T(8,128)S(1)} %get-tuple-element.27.second_ref, f32[256,128]{1,0:T(8,128)S(1)} %collective-permute-done.4.second_in_ref, ...), custom_call_target="tpu_custom_call" | custom-call | tf_op jit(solution)/shard_map/modes/pallas_call | solution.py:439
  24.0 0.2 collective-permute-start.5
  24.3 0.4 collective-permute-start.6
  24.6 1.0 %collective-permute-done.6.b_ref = f32[8,128]{1,0:T(8,128)S(1)} collective-permute-done((f32[8,128]{1,0:T(8,128)S(1)}, f32[8,128]{1,0:T(8,128)S(1)}, u32[]{:S(2)}, u32[]{:S(2)}) %collective-permute-start.6) | collective-permute-done | bytes 4128 | tf_op jit(solution)/shard_map/ppermute | solution.py:451
  25.7 0.0 collective-permute-done.5.other_ref.after_ref
  25.7 0.7 %spread.1 = f32[32,8,128]{2,1,0:T(8,128)} custom-call(f32[8,128]{1,0:T(8,128)S(1)} %get-tuple-element.32.a_ref, f32[8,128]{1,0:T(8,128)S(1)} %collective-permute-done.6.b_ref, f32[64,1024]{1,0:T(8,128)S(1)} %collective-permute-done.5.other_ref.after_ref), custom_call_target="tpu_custom_call" | custom-call | tf_op jit(solution)/shard_map/spread/pallas_call | solution.py:453
  26.3 10.6 %all-to-all-start = ((f32[32,8,128]{2,1,0:T(8,128)}), f32[32,8,128]{2,1,0:T(8,128)S(1)}, u32[]{:S(2)}, u32[]{:S(2)}) async-start(f32[32,8,128]{2,1,0:T(8,128)} %spread.1), calls=%async_computation | async-start | bytes 262144 | tf_op jit(solution)/shard_map/all_to_all | solution.py:461
  36.9 4.3 %misfit.1 = (f32[64,2048]{1,0:T(8,128)}, f32[2048,512]{1,0:T(8,128)}, f32[8,128]{1,0:T(8,128)S(1)}) custom-call(f32[2048,512]{1,0:T(8,128)} %d_hbm.3, f32[64,1024]{1,0:T(8,128)S(1)} %get-tuple-element.29.own_ref, f32[64,1024]{1,0:T(8,128)S(1)} %collective-permute-done.5.other_ref.after_ref, bf16[512,256]{1,0:T(8,128)(2,1)S(1)} %get-tuple-element.21.w_ref), custom_call_target="tpu_custom_call" | custom-call | flops 1000000000 | bytes 10000000 | tf_op jit(solution)/shard_map/misfit/pallas_call | solution.py:463
  41.2 5.1 %all-to-all-done.messages_ref = f32[32,8,128]{2,1,0:T(8,128)S(1)} async-done(((f32[32,8,128]{2,1,0:T(8,128)}), f32[32,8,128]{2,1,0:T(8,128)S(1)}, u32[]{:S(2)}, u32[]{:S(2)}) %all-to-all-start) | async-done | bytes 131104 | tf_op jit(solution)/shard_map/all_to_all | solution.py:461
  46.3 1.2 %collective-permute-start.7 = (f32[32,128]{1,0:T(8,128)S(1)}, f32[32,128]{1,0:T(8,128)S(1)}, u32[]{:S(2)}, u32[]{:S(2)}) collective-permute-start(f32[32,128]{1,0:T(8,128)S(1)} %collect.1), channel_id=1, source_target_pairs={{0,3},{1,2},{2,1},{3,0},{4,7},{5,6},{6,5},{7,4},{8,11},{9,10},{10,... | collective-permute-start | bytes 49160 | tf_op jit(solution)/shard_map/ppermute | solution.py:485
  47.5 2.0 %collective-permute-done.7 = f32[32,128]{1,0:T(8,128)S(1)} collective-permute-done((f32[32,128]{1,0:T(8,128)S(1)}, f32[32,128]{1,0:T(8,128)S(1)}, u32[]{:S(2)}, u32[]{:S(2)}) %collective-permute-start.7) | collective-permute-done | bytes 16416 | tf_op jit(solution)/shard_map/ppermute | solution.py:485
  49.6 3.4 %collective-permute-start.8 = (f32[32,128]{1,0:T(8,128)S(1)}, f32[32,128]{1,0:T(8,128)S(1)}, u32[]{:S(2)}, u32[]{:S(2)}) collective-permute-start(f32[32,128]{1,0:T(8,128)S(1)} %add.15.refs_0_), channel_id=1, source_target_pairs={{0,7},{1,6},{2,5},{3,4},{4,3},{5,2},{6,1},{7,0},{8,15},{9,14},{10,... | collective-permute-start | bytes 49160 | tf_op jit(solution)/shard_map/ppermute | solution.py:486
  52.9 1.4 %collective-permute-done.8.refs_1_ = f32[32,128]{1,0:T(8,128)S(1)} collective-permute-done((f32[32,128]{1,0:T(8,128)S(1)}, f32[32,128]{1,0:T(8,128)S(1)}, u32[]{:S(2)}, u32[]{:S(2)}) %collective-permute-start.8) | collective-permute-done | bytes 16416 | tf_op jit(solution)/shard_map/ppermute | solution.py:486
  54.4 1.0 %newton.1 = (f32[1,64]{1,0:T(1,128)}, f32[64,64]{1,0:T(8,128)}) custom-call(f32[32,128]{1,0:T(8,128)S(1)} %add.15.refs_0_, f32[32,128]{1,0:T(8,128)S(1)} %collective-permute-done.8.refs_1_, f32[4,64,128]{2,1,0:T(8,128)S(1)} %get-tuple-element.34.refs_2_, f32[64,128]{1,0:T(8,128)S(1)} %get-tuple-element.35.refs_3_), custom_call_target="tpu_custom_call" | custom-call | tf_op jit(solution)/shard_map/newton/pallas_call | solution.py:487
  (5 shorter events, 0.1 us)
Async XLA Ops:
  3.0 5.7 %collective-permute-start = (f32[1024,128]{1,0:T(8,128)S(1)}, f32[1024,128]{1,0:T(8,128)S(1)}, u32[]{:S(2)}, u32[]{:S(2)}) collective-permute-start(f32[1024,128]{1,0:T(8,128)S(1)} %get-tuple-element.22), channel_id=1, source_target_pairs={{0,1},{1,0},{2,3},{3,2},{4,5},{5,4},{6,7},{7,6},{8,9},{9,8},{10,11... | collective-permute-start | bytes 1572872 | tf_op jit(solution)/shard_map/ppermute | solution.py:396
  8.8 6.4 %collective-permute-start.2 = (f32[256,128]{1,0:T(8,128)S(1)}, f32[256,128]{1,0:T(8,128)S(1)}, u32[]{:S(2)}, u32[]{:S(2)}) collective-permute-start(f32[256,128]{1,0:T(8,128)S(1)} %get-tuple-element.40), channel_id=1, source_target_pairs={{0,7},{1,6},{2,5},{3,4},{4,3},{5,2},{6,1},{7,0},{8,15},{9,14},{10,... | collective-permute-start | bytes 393224 | tf_op jit(solution)/shard_map/ppermute | solution.py:413
  9.8 5.7 %collective-permute-start.1 = (f32[256,128]{1,0:T(8,128)S(1)}, f32[256,128]{1,0:T(8,128)S(1)}, u32[]{:S(2)}, u32[]{:S(2)}) collective-permute-start(f32[256,128]{1,0:T(8,128)S(1)} %get-tuple-element.41), channel_id=1, source_target_pairs={{0,3},{1,2},{2,1},{3,0},{4,7},{5,6},{6,5},{7,4},{8,11},{9,10},{10,... | collective-permute-start | bytes 393224 | tf_op jit(solution)/shard_map/ppermute | solution.py:412
  15.5 6.8 %collective-permute-start.3 = (f32[256,128]{1,0:T(8,128)S(1)}, f32[256,128]{1,0:T(8,128)S(1)}, u32[]{:S(2)}, u32[]{:S(2)}) collective-permute-start(f32[256,128]{1,0:T(8,128)S(1)} %get-tuple-element.26.after_ref.first_ref), channel_id=1, source_target_pairs={{0,7},{1,6},{2,5},{3,4},{4,3},{5,2},{6,1},{7,0},{8,15},{9,14},{10,... | collective-permute-start | bytes 393224 | tf_op jit(solution)/shard_map/ppermute | solution.py:428
  17.6 5.2 %collective-permute-start.4 = (f32[256,128]{1,0:T(8,128)S(1)}, f32[256,128]{1,0:T(8,128)S(1)}, u32[]{:S(2)}, u32[]{:S(2)}) collective-permute-start(f32[256,128]{1,0:T(8,128)S(1)} %get-tuple-element.27.second_ref), channel_id=1, source_target_pairs={{0,3},{1,2},{2,1},{3,0},{4,7},{5,6},{6,5},{7,4},{8,11},{9,10},{10,... | collective-permute-start | bytes 393224 | tf_op jit(solution)/shard_map/ppermute | solution.py:429
  24.0 1.6 %collective-permute-start.5 = (f32[64,1024]{1,0:T(8,128)S(1)}, f32[64,1024]{1,0:T(8,128)S(1)}, u32[]{:S(2)}, u32[]{:S(2)}) collective-permute-start(f32[64,1024]{1,0:T(8,128)S(1)} %get-tuple-element.29.own_ref), channel_id=1, source_target_pairs={{0,1},{1,0},{2,3},{3,2},{4,5},{5,4},{6,7},{7,6},{8,9},{9,8},{10,11... | collective-permute-start | bytes 786440 | tf_op jit(solution)/shard_map/ppermute | solution.py:452
  24.3 1.4 %collective-permute-start.6 = (f32[8,128]{1,0:T(8,128)S(1)}, f32[8,128]{1,0:T(8,128)S(1)}, u32[]{:S(2)}, u32[]{:S(2)}) collective-permute-start(f32[8,128]{1,0:T(8,128)S(1)} %get-tuple-element.32.a_ref), channel_id=1, source_target_pairs={{0,1},{1,0},{2,3},{3,2},{4,5},{5,4},{6,7},{7,6},{8,9},{9,8},{10,11... | collective-permute-start | bytes 12296 | tf_op jit(solution)/shard_map/ppermute | solution.py:451
  26.3 19.9 %all-to-all-start = ((f32[32,8,128]{2,1,0:T(8,128)}), f32[32,8,128]{2,1,0:T(8,128)S(1)}, u32[]{:S(2)}, u32[]{:S(2)}) async-start(f32[32,8,128]{2,1,0:T(8,128)} %spread.1), calls=%async_computation | async-start | bytes 262144 | tf_op jit(solution)/shard_map/all_to_all | solution.py:461
  46.3 3.2 %collective-permute-start.7 = (f32[32,128]{1,0:T(8,128)S(1)}, f32[32,128]{1,0:T(8,128)S(1)}, u32[]{:S(2)}, u32[]{:S(2)}) collective-permute-start(f32[32,128]{1,0:T(8,128)S(1)} %collect.1), channel_id=1, source_target_pairs={{0,3},{1,2},{2,1},{3,0},{4,7},{5,6},{6,5},{7,4},{8,11},{9,10},{10,... | collective-permute-start | bytes 49160 | tf_op jit(solution)/shard_map/ppermute | solution.py:485
  49.6 4.8 %collective-permute-start.8 = (f32[32,128]{1,0:T(8,128)S(1)}, f32[32,128]{1,0:T(8,128)S(1)}, u32[]{:S(2)}, u32[]{:S(2)}) collective-permute-start(f32[32,128]{1,0:T(8,128)S(1)} %add.15.refs_0_), channel_id=1, source_target_pairs={{0,7},{1,6},{2,5},{3,4},{4,3},{5,2},{6,1},{7,0},{8,15},{9,14},{10,... | collective-permute-start | bytes 49160 | tf_op jit(solution)/shard_map/ppermute | solution.py:486

commit v3 on v2

--- a/solution.py
+++ b/solution.py
@@ -81,25 +81,22 @@
     return copies
 
 
-def project(copies, buf, w, out_ref):
-    width = out_ref.shape[1]
+def project(d, w):
+    width = w.shape[1] // 2
     half = width // 2
-    count = out_ref.shape[0] // 2
-    for copy in copies:
-        copy.wait()
+    count = d.shape[0] // 2
 
     def product(start):
-        hi, lo = split(buf[start : start + count, :])
+        hi, lo = split(d[start : start + count, :])
         both = dot(hi, w) + dot(lo, w)
         return both[:, :width] + both[:, width:]
 
     x, y = product(0), product(count)
     left = lax.broadcasted_iota(jnp.int32, x.shape, 1) < half
-    out_ref[:count, :] = jnp.where(left, x, pltpu.roll(y, half, 1))
-    out_ref[count:, :] = jnp.where(left, pltpu.roll(x, half, 1), y)
-
-
-def first_kernel(complete, d_hbm, rates_hbm, freqs_hbm, out_ref, w_ref, rates_ref, freqs_ref, buf, sems, psems):
+    return jnp.where(left, x, pltpu.roll(y, half, 1)), jnp.where(left, pltpu.roll(x, half, 1), y)
+
+
+def first_kernel(complete, d_hbm, rates_hbm, freqs_hbm, out_ref, product_ref, w_ref, rates_ref, freqs_ref, buf, sems, psems):
     tm = lax.axis_index("tm")
     rates_copy = pltpu.make_async_copy(rates_hbm, rates_ref, psems.at[0])
     freqs_copy = pltpu.make_async_copy(freqs_hbm, freqs_ref, psems.at[1])
@@ -117,12 +114,21 @@
     hi, lo = split(x)
     w_ref[:, :width] = hi
     w_ref[:, width:] = lo
-    project(copies, buf, w_ref[...], out_ref)
-
-
-def second_kernel(d_hbm, w_ref, out_ref, buf, sems):
-    copies = load_half(d_hbm, buf, sems, half_index(lax.axis_index("tm")))
-    project(copies, buf, w_ref[...], out_ref)
+    for copy in copies:
+        copy.wait()
+    projection, product = project(buf, w_ref[...])
+    out_ref[...] = projection
+    product_ref[...] = product
+
+
+def second_kernel(d_ref, w_ref, first_ref, second_ref, product_ref):
+    half = d_ref.shape[0] // 2
+    start = half_index(lax.axis_index("tm")) * half
+    projection, product = project(d_ref.at[pl.ds(pl.multiple_of(start, half), half)], w_ref[...])
+    count = first_ref.shape[0]
+    first_ref[...] = projection[:count]
+    second_ref[...] = projection[count:]
+    product_ref[...] = product
 
 
 def swap_rows(x):
@@ -184,12 +190,17 @@
     return a
 
 
+def dot_tn(a, b):
+    return lax.dot_general(a, b, (((0,), (0,)), ((), ())), preferred_element_type=f32)
+
+
 def gram_kernel(complete, rates_ref, freqs_ref, after_ref, gram_ref, slope_ref, basis_slope_ref):
     del after_ref
     width = 4 * rates_ref.shape[1]
     half = width // 2
     rates, freqs = rates_ref[...], freqs_ref[...]
-    total = jnp.zeros((2 * width, 2 * width), f32)
+    with_basis = jnp.zeros((2 * width, 4 * width), f32)
+    with_slope = jnp.zeros((2 * width, 2 * width), f32)
     block = 512
     rows = lax.broadcasted_iota(jnp.int32, (block, width), 0)
     lanes = lax.broadcasted_iota(jnp.int32, (block, width), 1)
@@ -197,18 +208,18 @@
     for i in range(complete // 2 // block):
         t = (start + i * block).astype(f32) / complete
         x = decayed_waves(rates, freqs, t)
-        x = jnp.concatenate([x, x * t], axis=1)
-        total = total + lax.dot_general(
-            x, x, (((0,), (0,)), ((), ())), precision=highest, preferred_element_type=f32
-        )
-
-    def fold(i, j):
-        block = total[i * width : (i + 1) * width, j * width : (j + 1) * width]
+        z = jnp.concatenate([*split(x), *split(x * t)], axis=1)
+        with_basis = with_basis + dot_tn(z[:, : 2 * width], z)
+        with_slope = with_slope + dot_tn(z[:, 2 * width :], z[:, 2 * width :])
+
+    def fold(total, j):
+        block = total[:, j : j + width] + total[:, j + width : j + 2 * width]
+        block = block[:width] + block[width:]
         return block[:half] + pltpu.roll(block[half:], half, 1)
 
-    gram_ref[...] = fold(0, 0)
-    basis_slope_ref[...] = fold(0, 1)
-    slope = fold(1, 1)
+    gram_ref[...] = fold(with_basis, 0)
+    basis_slope_ref[...] = fold(with_basis, 2 * width)
+    slope = fold(with_slope, 0)
     lanes = lax.broadcasted_iota(jnp.int32, slope.shape, 1)
     rows = lax.broadcasted_iota(jnp.int32, slope.shape, 0)
     row_sign = jnp.where(rows % 2 == 0, -1.0, 1.0)
@@ -225,19 +236,27 @@
     half, width = gram_ref.shape
     inv = inverse(gram_ref[...])
     inv = jnp.where(lax.broadcasted_iota(jnp.int32, inv.shape, 1) < half, inv, 0.0)
-    inverse_ref[:half] = inv
-    inverse_ref[half:] = pltpu.roll(inv, half, 1)
-
-
-def modes_kernel(first_ref, first_in_ref, second_ref, second_in_ref, product_ref, inverse_ref, modes_ref, message_ref):
+    inv = jnp.concatenate([inv, pltpu.roll(inv, half, 1)], axis=0)
+    one, two = split(inv)
+    three = (inv - one.astype(f32) - two.astype(f32)).astype(bf16)
+    twice = jnp.concatenate([one, two], axis=1)
+    inverse_ref[:width] = twice
+    inverse_ref[width : 2 * width] = twice
+    inverse_ref[2 * width :] = jnp.concatenate([three, jnp.zeros_like(three)], axis=1)
+
+
+def modes_kernel(first_ref, first_in_ref, second_ref, second_in_ref, product_ref, product_in_ref, inverse_ref, modes_ref, message_ref):
     x = jnp.concatenate([first_ref[...] + first_in_ref[...], second_ref[...] + second_in_ref[...]], axis=0)
-    x = dot(x, inverse_ref[...], highest)
-    count, width = x.shape
+    width = x.shape[1]
+    hi, lo = split(x)
+    both = dot(jnp.concatenate([hi, lo], axis=1), inverse_ref[: 2 * width])
+    x = both[:, :width] + (both[:, width:] + dot(hi, inverse_ref[2 * width :, :width]))
+    count = x.shape[0]
     half, quarter = width // 2, width // 4
     flat = jnp.transpose(x)
     modes_ref[:, :count] = flat[:half]
     modes_ref[:, count:] = flat[half:]
-    both = dot(flat, jnp.concatenate([x, product_ref[...]], axis=1), highest)
+    both = dot(flat, jnp.concatenate([x, product_ref[...] + product_in_ref[...]], axis=1), highest)
     gram = both[:half, :width] + pltpu.roll(both[half:, :width], half, 1)
     cross = both[:half, width:] + pltpu.roll(both[half:, width:], half, 1)
     rows = lax.broadcasted_iota(jnp.int32, cross.shape, 0)
@@ -379,36 +398,37 @@
     slab = in_hbm(frame_slab)
     scratch = [pltpu.VMEM((half, epochs), f32), pltpu.SemaphoreType.DMA((4,))]
 
-    away, w, rates, freqs = pl.pallas_call(
+    away, product_away, w, rates, freqs = pl.pallas_call(
         lambda *refs: first_kernel(complete, *refs),
         out_shape=(
-            jax.ShapeDtypeStruct((half, width), f32),
+            jax.ShapeDtypeStruct((quarter, width), f32),
+            jax.ShapeDtypeStruct((quarter, width), f32),
             jax.ShapeDtypeStruct((epochs, 2 * width), bf16),
             jax.ShapeDtypeStruct((1, pairs), f32),
             jax.ShapeDtypeStruct((1, pairs), f32),
         ),
         in_specs=[HBM, HBM, HBM],
-        out_specs=(VMEM,) * 4,
+        out_specs=(VMEM,) * 5,
         scratch_shapes=scratch + [pltpu.SemaphoreType.DMA((2,))],
         compiler_params=PARAMS,
         name="project_away",
     )(slab, rates, freqs)
     arrived = lax.ppermute(away, "tm", flips(tm_size, 1))
-    kept = pl.pallas_call(
+    eighth = quarter // 2
+    first, second, product = pl.pallas_call(
         second_kernel,
-        out_shape=jax.ShapeDtypeStruct((half, width), f32),
-        in_specs=[HBM, VMEM],
-        out_specs=VMEM,
-        scratch_shapes=scratch,
+        out_shape=[jax.ShapeDtypeStruct((n, width), f32) for n in (eighth, eighth, quarter)],
+        in_specs=[VMEM, VMEM],
+        out_specs=[VMEM] * 3,
         compiler_params=PARAMS,
         cost_estimate=cost(2 * half * epochs * width * 4, half * epochs * 4),
         name="project_kept",
-    )(slab, w)
+    )(frame_slab, w)
 
     near, wrap = flips(tm_size, 3), flips(tm_size, 7)
-    summed = kept + arrived
-    eighth = quarter // 2
-    first, second, product = summed[:eighth], summed[eighth:quarter], summed[quarter:]
+    first, second = first + arrived[:eighth], second + arrived[eighth:]
+    product_away, first, second = lax.optimization_barrier((product_away, first, second))
+    product_in = lax.ppermute(product_away, "tm", flips(tm_size, 1))
     first_in = lax.ppermute(first, "tm", near)
     second_in = lax.ppermute(second, "tm", wrap)
     gram, slopes, basis_slope = pl.pallas_call(
@@ -423,30 +443,32 @@
         compiler_params=PARAMS,
         cost_estimate=cost(10**9, 10**7),
         name="grams",
-    )(rates, freqs, kept)
-    first, second, gram = lax.optimization_barrier((first + first_in, second + second_in, gram))
+    )(rates, freqs, product)
+    first, gram = lax.optimization_barrier((first + first_in, gram))
     first_in = lax.ppermute(first, "tm", wrap)
+    second, first = lax.optimization_barrier((second, first))
+    second = second + second_in
     second_in = lax.ppermute(second, "tm", near)
     inverse_gram = pl.pallas_call(
         inverse_kernel,
-        out_shape=jax.ShapeDtypeStruct((width, width), f32),
+        out_shape=jax.ShapeDtypeStruct((3 * width, 2 * width), bf16),
         in_specs=[VMEM, ANY],
         out_specs=VMEM,
         compiler_params=PARAMS,
         cost_estimate=cost(10**9, 10**7),
         name="inverse",
-    )(gram, first)
+    )(gram, second)
     modes_half, message = pl.pallas_call(
         modes_kernel,
         out_shape=(
             jax.ShapeDtypeStruct((basis, half), f32),
             jax.ShapeDtypeStruct((8, width), f32),
         ),
-        in_specs=[VMEM] * 6,
+        in_specs=[VMEM] * 7,
         out_specs=(VMEM, VMEM),
         compiler_params=PARAMS,
         name="modes",
-    )(first, first_in, second, second_in, product, inverse_gram)
+    )(first, first_in, second, second_in, product, product_in, inverse_gram)
 
     message_in = lax.ppermute(message, "tm", flips(tm_size, 1))
     modes_other = lax.ppermute(modes_half, "tm", flips(tm_size, 1))
@@ -458,7 +480,7 @@
         compiler_params=PARAMS,
         name="spread",
     )(message, message_in, modes_other)
-    messages = lax.all_to_all(messages, "space", 0, 0)
+    messages = lax.all_to_all(messages, "space", 0, 0, axis_index_groups=[list(range(space_size))[::-1]])
     blocks = 8
     spatial_modes, misfit, done = pl.pallas_call(
         misfit_kernel,

time: 55.5 us -> 49.8 us (0.90)
  waiting for transfers between devices: 13.5 us -> 9.69 us
  Pallas kernels: 18.6 us -> 15.7 us
  starting transfers between devices: 22.4 us -> 23.5 us
    all_to_all x1, waiting for transfers between devices: 5.06 us -> 1.24 us  [local(): lax.all_to_all(messages, 'space', 0, 0, axis_index_groups=[list(range(spa...]
    pallas_call x2, Pallas kernels: 5.26 us -> 3.69 us  [the longest x1 2.89 us: local(): pl.pallas_call(inverse_kernel, out_shape=jax.ShapeDtypeStruct((3 * width,...]
    ppermute x1, waiting for transfers between devices: 1.36 us -> 0.01 us  [local(): second_in = lax.ppermute(second, 'tm', wrap)]
    pallas_call x1, Pallas kernels: 3.83 us -> 2.5 us  [local(): pl.pallas_call(lambda *refs: gram_kernel(complete, *refs), out_shape=(jax...]
    all_to_all x1, starting transfers between devices: 10.6 us -> 11.8 us  [local(): lax.all_to_all(messages, 'space', 0, 0, axis_index_groups=[list(range(spa...]
    ppermute x1, starting transfers between devices: 2.05 us -> 1.05 us  [local(): first_in = lax.ppermute(first, 'tm', wrap)]
    ppermute x1, waiting for transfers between devices: 0.25 us -> 1.15 us  [local(): first_in = lax.ppermute(first, 'tm', near)]
    ppermute x1, starting transfers between devices: 0.99 us -> 1.74 us  [local(): second_in = lax.ppermute(second, 'tm', wrap)]
  transfers between devices with their start and end apart: 10 -> 11, of which waited for: 8 -> 8; matrix products, arithmetic and copies ran while one was open for 0% -> 0% of each run, Pallas kernels for 24% -> 21%
where the time goes in v3:
time: 49.8 us; the launch traced here: 49.6 us
  starting transfers between devices  23.5 us (47%)
  Pallas kernels  15.7 us (32%)
  waiting for transfers between devices  9.69 us (19%)
  between operations  0.72 us (1%)
    all_to_all x1, starting transfers between devices, local(): lax.all_to_all(messages, 'space', 0, 0, axis_index_groups=[list(range(spa...  11.8 us
    pallas_call x1, Pallas kernels, local(): pl.pallas_call(misfit_kernel, out_shape=(jax.ShapeDtypeStruct((basis, poi...  4.28 us
    ppermute x1, starting transfers between devices, local(): arrived = lax.ppermute(away, 'tm', flips(tm_size, 1))  3.33 us
    pallas_call x1, Pallas kernels, local(): pl.pallas_call(inverse_kernel, out_shape=jax.ShapeDtypeStruct((3 * width,...  2.89 us
    ppermute x1, starting transfers between devices, local(): total_in = lax.ppermute(total, 'tm', wrap)  2.68 us
    pallas_call x1, Pallas kernels, local(): pl.pallas_call(lambda *refs: first_kernel(complete, *refs), out_shape=(ja...  2.54 us
    pallas_call x1, Pallas kernels, local(): pl.pallas_call(lambda *refs: gram_kernel(complete, *refs), out_shape=(jax...  2.5 us
    ppermute x1, waiting for transfers between devices, local(): first_in = lax.ppermute(first, 'tm', wrap)  2.19 us
  transfers between devices with their start and end apart: 11, of which 8 were waited for; matrix products, arithmetic and copies ran while one was open for 0% of the time, Pallas kernels for 21%

profile of v3, /device:TPU:1, one launch (start us, length us, event | category | flops | bytes accessed | tf_op | source)
XLA Modules:
  0.0 49.6 jit_solution(17455880543737040141)
XLA Ops:
  0.6 0.0 copy-start
  0.6 2.5 %project_away.1 = (f32[512,128]{1,0:T(8,128)S(1)}, f32[512,128]{1,0:T(8,128)S(1)}, bf16[512,256]{1,0:T(8,128)(2,1)S(1)}, f32[1,32]{1,0:T(1,128)S(1)}, f32[1,32]{1,0:T(1,128)S(1)}) custom-call(f32[2048,512]{1,0:T(8,128)} %d_hbm.1, f32[1,32]{1,0:T(1,128)} %bitcast.3, f32[1,32]{1,0:T(1,128)} %bitcast.4), custom_call_target="tpu_custom_call" | custom-call | tf_op jit(solution)/shard_map/project_away/pallas_call | solution.py:401
  3.2 3.3 %collective-permute-start = (f32[512,128]{1,0:T(8,128)S(1)}, f32[512,128]{1,0:T(8,128)S(1)}, u32[]{:S(2)}, u32[]{:S(2)}) collective-permute-start(f32[512,128]{1,0:T(8,128)S(1)} %get-tuple-element.32), channel_id=1, source_target_pairs={{0,1},{1,0},{2,3},{3,2},{4,5},{5,4},{6,7},{7,6},{8,9},{9,8},{10,11... | collective-permute-start | bytes 786440 | tf_op jit(solution)/shard_map/ppermute | solution.py:416
  6.5 0.0 copy-done
  6.5 0.8 %project_kept.1 = (f32[256,128]{1,0:T(8,128)S(1)}, f32[256,128]{1,0:T(8,128)S(1)}, f32[512,128]{1,0:T(8,128)S(1)}) custom-call(f32[2048,512]{1,0:T(8,128)S(1)} %copy-done, bf16[512,256]{1,0:T(8,128)(2,1)S(1)} %get-tuple-element.30.w_ref), custom_call_target="tpu_custom_call" | custom-call | flops 536870912 | bytes 2097152 | tf_op jit(solution)/shard_map/project_kept/pallas_call | solution.py:418
  7.3 0.4 collective-permute-done
  7.7 0.1 collective-permute-start.1
  7.8 1.7 %collective-permute-start.3 = (f32[256,128]{1,0:T(8,128)S(1)}, f32[256,128]{1,0:T(8,128)S(1)}, u32[]{:S(2)}, u32[]{:S(2)}) collective-permute-start(f32[256,128]{1,0:T(8,128)S(1)} %get-tuple-element.42), channel_id=1, source_target_pairs={{0,7},{1,6},{2,5},{3,4},{4,3},{5,2},{6,1},{7,0},{8,15},{9,14},{10,... | collective-permute-start | bytes 393224 | tf_op jit(solution)/shard_map/ppermute | solution.py:433
  9.6 0.4 collective-permute-start.5
  9.9 2.5 %grams.1 = (f32[64,128]{1,0:T(8,128)S(1)}, f32[4,64,128]{2,1,0:T(8,128)S(1)}, f32[64,128]{1,0:T(8,128)S(1)}) custom-call(f32[1,32]{1,0:T(1,128)S(1)} %get-tuple-element.36.refs_0_, f32[1,32]{1,0:T(1,128)S(1)} %get-tuple-element.37.refs_1_, f32[512,128]{1,0:T(8,128)S(1)} %get-tuple-element.38.refs_2_.product_ref), custom_call_target="tpu_custom_call" | custom-call | flops 1000000000 | bytes 10000000 | tf_op jit(solution)/shard_map/grams/pallas_call | solution.py:434
  12.4 1.1 %collective-permute-done.1 = f32[256,128]{1,0:T(8,128)S(1)} collective-permute-done((f32[256,128]{1,0:T(8,128)S(1)}, f32[256,128]{1,0:T(8,128)S(1)}, u32[]{:S(2)}, u32[]{:S(2)}) %collective-permute-start.1) | collective-permute-done | bytes 131104 | tf_op jit(solution)/shard_map/ppermute | solution.py:432
  13.6 1.0 %collective-permute-start.2 = (f32[256,128]{1,0:T(8,128)S(1)}, f32[256,128]{1,0:T(8,128)S(1)}, u32[]{:S(2)}, u32[]{:S(2)}) collective-permute-start(f32[256,128]{1,0:T(8,128)S(1)} %add.17.first_ref), channel_id=1, source_target_pairs={{0,7},{1,6},{2,5},{3,4},{4,3},{5,2},{6,1},{7,0},{8,15},{9,14},{10,... | collective-permute-start | bytes 393224 | tf_op jit(solution)/shard_map/ppermute | solution.py:448
  14.7 0.0 collective-permute-done.3
  14.7 0.3 collective-permute-start.4
  15.0 2.9 %inverse.1.inverse_ref = bf16[384,256]{1,0:T(8,128)(2,1)S(1)} custom-call(f32[64,128]{1,0:T(8,128)S(1)} %get-tuple-element.44.gram_ref, f32[256,128]{1,0:T(8,128)S(1)} %add.18.after_ref.second_ref), custom_call_target="tpu_custom_call" | custom-call | flops 1000000000 | bytes 10000000 | tf_op jit(solution)/shard_map/inverse/pallas_call | solution.py:452
  17.9 2.2 %collective-permute-done.2.first_in_ref = f32[256,128]{1,0:T(8,128)S(1)} collective-permute-done((f32[256,128]{1,0:T(8,128)S(1)}, f32[256,128]{1,0:T(8,128)S(1)}, u32[]{:S(2)}, u32[]{:S(2)}) %collective-permute-start.2) | collective-permute-done | bytes 131104 | tf_op jit(solution)/shard_map/ppermute | solution.py:448
  20.1 0.3 collective-permute-done.4.second_in_ref
  20.4 0.0 collective-permute-done.5.product_in_ref
  20.4 1.0 %modes.1 = (f32[64,1024]{1,0:T(8,128)S(1)}, f32[8,128]{1,0:T(8,128)S(1)}) custom-call(f32[256,128]{1,0:T(8,128)S(1)} %add.17.first_ref, f32[256,128]{1,0:T(8,128)S(1)} %collective-permute-done.2.first_in_ref, f32[256,128]{1,0:T(8,128)S(1)} %add.18.after_ref.second_ref, f32[256,128]{1,0:T(8,128)S(1)} %collective-permute-done.4.second_in_ref, ...), custom_call_target="tpu_custom_call" | custom-call | tf_op jit(solution)/shard_map/modes/pallas_call | solution.py:461
  21.4 0.5 collective-permute-start.6
  21.9 0.1 collective-permute-start.7
  22.0 1.1 %collective-permute-done.7.b_ref = f32[8,128]{1,0:T(8,128)S(1)} collective-permute-done((f32[8,128]{1,0:T(8,128)S(1)}, f32[8,128]{1,0:T(8,128)S(1)}, u32[]{:S(2)}, u32[]{:S(2)}) %collective-permute-start.7) | collective-permute-done | bytes 4128 | tf_op jit(solution)/shard_map/ppermute | solution.py:473
  23.0 0.0 collective-permute-done.6.other_ref.after_ref
  23.0 0.7 %spread.1 = f32[32,8,128]{2,1,0:T(8,128)} custom-call(f32[8,128]{1,0:T(8,128)S(1)} %get-tuple-element.48.a_ref, f32[8,128]{1,0:T(8,128)S(1)} %collective-permute-done.7.b_ref, f32[64,1024]{1,0:T(8,128)S(1)} %collective-permute-done.6.other_ref.after_ref), custom_call_target="tpu_custom_call" | custom-call | tf_op jit(solution)/shard_map/spread/pallas_call | solution.py:475
  23.7 11.8 %all-to-all-start = ((f32[32,8,128]{2,1,0:T(8,128)}), f32[32,8,128]{2,1,0:T(8,128)S(1)}, u32[]{:S(2)}, u32[]{:S(2)}) async-start(f32[32,8,128]{2,1,0:T(8,128)} %spread.1), calls=%async_computation | async-start | bytes 262144 | tf_op jit(solution)/shard_map/all_to_all | solution.py:483
  35.5 4.3 %misfit.1 = (f32[64,2048]{1,0:T(8,128)}, f32[2048,512]{1,0:T(8,128)}, f32[8,128]{1,0:T(8,128)S(1)}) custom-call(f32[2048,512]{1,0:T(8,128)} %d_hbm.1, f32[64,1024]{1,0:T(8,128)S(1)} %get-tuple-element.45.own_ref, f32[64,1024]{1,0:T(8,128)S(1)} %collective-permute-done.6.other_ref.after_ref, bf16[512,256]{1,0:T(8,128)(2,1)S(1)} %get-tuple-element.30.w_ref), custom_call_target="tpu_custom_call" | custom-call | flops 1000000000 | bytes 10000000 | tf_op jit(solution)/shard_map/misfit/pallas_call | solution.py:485
  39.7 1.2 %all-to-all-done.messages_ref = f32[32,8,128]{2,1,0:T(8,128)S(1)} async-done(((f32[32,8,128]{2,1,0:T(8,128)}), f32[32,8,128]{2,1,0:T(8,128)S(1)}, u32[]{:S(2)}, u32[]{:S(2)}) %all-to-all-start) | async-done | bytes 131104 | tf_op jit(solution)/shard_map/all_to_all | solution.py:483
  41.0 1.5 %collective-permute-start.8 = (f32[32,128]{1,0:T(8,128)S(1)}, f32[32,128]{1,0:T(8,128)S(1)}, u32[]{:S(2)}, u32[]{:S(2)}) collective-permute-start(f32[32,128]{1,0:T(8,128)S(1)} %collect.1), channel_id=1, source_target_pairs={{0,3},{1,2},{2,1},{3,0},{4,7},{5,6},{6,5},{7,4},{8,11},{9,10},{10,... | collective-permute-start | bytes 49160 | tf_op jit(solution)/shard_map/ppermute | solution.py:507
  42.6 1.7 %collective-permute-done.8 = f32[32,128]{1,0:T(8,128)S(1)} collective-permute-done((f32[32,128]{1,0:T(8,128)S(1)}, f32[32,128]{1,0:T(8,128)S(1)}, u32[]{:S(2)}, u32[]{:S(2)}) %collective-permute-start.8) | collective-permute-done | bytes 16416 | tf_op jit(solution)/shard_map/ppermute | solution.py:507
  44.3 2.7 %collective-permute-start.9 = (f32[32,128]{1,0:T(8,128)S(1)}, f32[32,128]{1,0:T(8,128)S(1)}, u32[]{:S(2)}, u32[]{:S(2)}) collective-permute-start(f32[32,128]{1,0:T(8,128)S(1)} %add.19.refs_0_), channel_id=1, source_target_pairs={{0,7},{1,6},{2,5},{3,4},{4,3},{5,2},{6,1},{7,0},{8,15},{9,14},{10,... | collective-permute-start | bytes 49160 | tf_op jit(solution)/shard_map/ppermute | solution.py:508
  47.0 1.7 %collective-permute-done.9.refs_1_ = f32[32,128]{1,0:T(8,128)S(1)} collective-permute-done((f32[32,128]{1,0:T(8,128)S(1)}, f32[32,128]{1,0:T(8,128)S(1)}, u32[]{:S(2)}, u32[]{:S(2)}) %collective-permute-start.9) | collective-permute-done | bytes 16416 | tf_op jit(solution)/shard_map/ppermute | solution.py:508
  48.7 1.0 %newton.1 = (f32[1,64]{1,0:T(1,128)}, f32[64,64]{1,0:T(8,128)}) custom-call(f32[32,128]{1,0:T(8,128)S(1)} %add.19.refs_0_, f32[32,128]{1,0:T(8,128)S(1)} %collective-permute-done.9.refs_1_, f32[4,64,128]{2,1,0:T(8,128)S(1)} %get-tuple-element.50.refs_2_, f32[64,128]{1,0:T(8,128)S(1)} %get-tuple-element.51.refs_3_), custom_call_target="tpu_custom_call" | custom-call | tf_op jit(solution)/shard_map/newton/pallas_call | solution.py:509
  (5 shorter events, 0.1 us)
Async XLA Ops:
  0.6 5.9 %copy-start = (f32[2048,512]{1,0:T(8,128)S(1)}, f32[2048,512]{1,0:T(8,128)}, u32[]{:S(2)}) copy-start(f32[2048,512]{1,0:T(8,128)} %d_hbm.1) | copy-start | bytes 12582916
  3.2 4.5 %collective-permute-start = (f32[512,128]{1,0:T(8,128)S(1)}, f32[512,128]{1,0:T(8,128)S(1)}, u32[]{:S(2)}, u32[]{:S(2)}) collective-permute-start(f32[512,128]{1,0:T(8,128)S(1)} %get-tuple-element.32), channel_id=1, source_target_pairs={{0,1},{1,0},{2,3},{3,2},{4,5},{5,4},{6,7},{7,6},{8,9},{9,8},{10,11... | collective-permute-start | bytes 786440 | tf_op jit(solution)/shard_map/ppermute | solution.py:416
  7.7 5.9 %collective-permute-start.1 = (f32[256,128]{1,0:T(8,128)S(1)}, f32[256,128]{1,0:T(8,128)S(1)}, u32[]{:S(2)}, u32[]{:S(2)}) collective-permute-start(f32[256,128]{1,0:T(8,128)S(1)} %get-tuple-element.35), channel_id=1, source_target_pairs={{0,3},{1,2},{2,1},{3,0},{4,7},{5,6},{6,5},{7,4},{8,11},{9,10},{10,... | collective-permute-start | bytes 393224 | tf_op jit(solution)/shard_map/ppermute | solution.py:432
  7.8 6.8 %collective-permute-start.3 = (f32[256,128]{1,0:T(8,128)S(1)}, f32[256,128]{1,0:T(8,128)S(1)}, u32[]{:S(2)}, u32[]{:S(2)}) collective-permute-start(f32[256,128]{1,0:T(8,128)S(1)} %get-tuple-element.42), channel_id=1, source_target_pairs={{0,7},{1,6},{2,5},{3,4},{4,3},{5,2},{6,1},{7,0},{8,15},{9,14},{10,... | collective-permute-start | bytes 393224 | tf_op jit(solution)/shard_map/ppermute | solution.py:433
  9.6 10.8 %collective-permute-start.5 = (f32[512,128]{1,0:T(8,128)S(1)}, f32[512,128]{1,0:T(8,128)S(1)}, u32[]{:S(2)}, u32[]{:S(2)}) collective-permute-start(f32[512,128]{1,0:T(8,128)S(1)} %get-tuple-element.43), channel_id=1, source_target_pairs={{0,1},{1,0},{2,3},{3,2},{4,5},{5,4},{6,7},{7,6},{8,9},{9,8},{10,11... | collective-permute-start | bytes 786440 | tf_op jit(solution)/shard_map/ppermute | solution.py:431
  13.6 6.5 %collective-permute-start.2 = (f32[256,128]{1,0:T(8,128)S(1)}, f32[256,128]{1,0:T(8,128)S(1)}, u32[]{:S(2)}, u32[]{:S(2)}) collective-permute-start(f32[256,128]{1,0:T(8,128)S(1)} %add.17.first_ref), channel_id=1, source_target_pairs={{0,7},{1,6},{2,5},{3,4},{4,3},{5,2},{6,1},{7,0},{8,15},{9,14},{10,... | collective-permute-start | bytes 393224 | tf_op jit(solution)/shard_map/ppermute | solution.py:448
  14.7 5.7 %collective-permute-start.4 = (f32[256,128]{1,0:T(8,128)S(1)}, f32[256,128]{1,0:T(8,128)S(1)}, u32[]{:S(2)}, u32[]{:S(2)}) collective-permute-start(f32[256,128]{1,0:T(8,128)S(1)} %add.18.after_ref.second_ref), channel_id=1, source_target_pairs={{0,3},{1,2},{2,1},{3,0},{4,7},{5,6},{6,5},{7,4},{8,11},{9,10},{10,... | collective-permute-start | bytes 393224 | tf_op jit(solution)/shard_map/ppermute | solution.py:451
  21.4 1.7 %collective-permute-start.6 = (f32[64,1024]{1,0:T(8,128)S(1)}, f32[64,1024]{1,0:T(8,128)S(1)}, u32[]{:S(2)}, u32[]{:S(2)}) collective-permute-start(f32[64,1024]{1,0:T(8,128)S(1)} %get-tuple-element.45.own_ref), channel_id=1, source_target_pairs={{0,1},{1,0},{2,3},{3,2},{4,5},{5,4},{6,7},{7,6},{8,9},{9,8},{10,11... | collective-permute-start | bytes 786440 | tf_op jit(solution)/shard_map/ppermute | solution.py:474
  21.9 1.2 %collective-permute-start.7 = (f32[8,128]{1,0:T(8,128)S(1)}, f32[8,128]{1,0:T(8,128)S(1)}, u32[]{:S(2)}, u32[]{:S(2)}) collective-permute-start(f32[8,128]{1,0:T(8,128)S(1)} %get-tuple-element.48.a_ref), channel_id=1, source_target_pairs={{0,1},{1,0},{2,3},{3,2},{4,5},{5,4},{6,7},{7,6},{8,9},{9,8},{10,11... | collective-permute-start | bytes 12296 | tf_op jit(solution)/shard_map/ppermute | solution.py:473
  23.7 17.3 %all-to-all-start = ((f32[32,8,128]{2,1,0:T(8,128)}), f32[32,8,128]{2,1,0:T(8,128)S(1)}, u32[]{:S(2)}, u32[]{:S(2)}) async-start(f32[32,8,128]{2,1,0:T(8,128)} %spread.1), calls=%async_computation | async-start | bytes 262144 | tf_op jit(solution)/shard_map/all_to_all | solution.py:483
  41.0 3.2 %collective-permute-start.8 = (f32[32,128]{1,0:T(8,128)S(1)}, f32[32,128]{1,0:T(8,128)S(1)}, u32[]{:S(2)}, u32[]{:S(2)}) collective-permute-start(f32[32,128]{1,0:T(8,128)S(1)} %collect.1), channel_id=1, source_target_pairs={{0,3},{1,2},{2,1},{3,0},{4,7},{5,6},{6,5},{7,4},{8,11},{9,10},{10,... | collective-permute-start | bytes 49160 | tf_op jit(solution)/shard_map/ppermute | solution.py:507
  44.3 4.4 %collective-permute-start.9 = (f32[32,128]{1,0:T(8,128)S(1)}, f32[32,128]{1,0:T(8,128)S(1)}, u32[]{:S(2)}, u32[]{:S(2)}) collective-permute-start(f32[32,128]{1,0:T(8,128)S(1)} %add.19.refs_0_), channel_id=1, source_target_pairs={{0,7},{1,6},{2,5},{3,4},{4,3},{5,2},{6,1},{7,0},{8,15},{9,14},{10,... | collective-permute-start | bytes 49160 | tf_op jit(solution)/shard_map/ppermute | solution.py:508

commit v4 on v3

--- a/solution.py
+++ b/solution.py
@@ -294,10 +294,7 @@
     total = messages_ref[0]
     for i in range(1, messages_ref.shape[0]):
         total = total + messages_ref[i]
-    y = lax.axis_index("tm") // 2
-    n = total.shape[0]
-    for i in range(out_ref.shape[0] // n):
-        out_ref[i * n : (i + 1) * n] = jnp.where(y == i, total, 0.0)
+    out_ref[...] = total
 
 
 def misfit_kernel(d_hbm, own_ref, other_ref, w_ref, modes_hbm, misfit_hbm, done_ref, out_ref, in_sems, sems, modes_sems):
@@ -336,8 +333,17 @@
     done_ref[...] = jnp.zeros_like(done_ref)
 
 
-def last_kernel(divisor, a_ref, b_ref, slope_ref, basis_slope_ref, gradient_ref, newton_ref):
-    total = a_ref[...] + b_ref[...]
+def last_kernel(divisor, own_ref, near_ref, far_ref, slope_ref, basis_slope_ref, gradient_ref, newton_ref):
+    y = lax.axis_index("tm") // 2
+    n = own_ref.shape[0]
+    shares = [(0, own_ref[...]), (1, near_ref[...]), (3, far_ref[:n]), (2, far_ref[n:])]
+    tiles = []
+    for i in range(4):
+        tile = shares[0][1]
+        for offset, share in shares[1:]:
+            tile = jnp.where((y ^ offset) == i, share, tile)
+        tiles.append(tile)
+    total = jnp.concatenate(tiles, axis=0)
     width = total.shape[1]
     half, quarter, eighth = width // 2, width // 4, width // 8
     share = (eighth + eighth // 2) // 4
@@ -354,23 +360,20 @@
     lanes = lax.broadcasted_iota(jnp.int32, (half, width), 1)
     gram = jnp.where(rows <= lanes, wide[:half], jnp.transpose(wide)[:half])
 
-    def block_sums(x):
-        y = x + swap_rows(x)
-        return y + swap_lanes(y)
-
-    def for_row(first, second):
-        return jnp.where(rows % 2 == 0, first, second)
-
-    even = for_row(block_sums(gram * slope_ref[0]), block_sums(gram * slope_ref[2]))
-    odd = for_row(block_sums(gram * slope_ref[1]), block_sums(gram * slope_ref[3]))
-    newton = divisor * jnp.where(lanes % 2 == 0, even, odd)
+    def pair_rows(first, second):
+        x, y = gram * first, gram * second
+        return jnp.where(rows % 2 == 0, x + pltpu.roll(x, half - 1, 0), y + pltpu.roll(y, 1, 0))
+
+    even = pair_rows(slope_ref[0], slope_ref[2])
+    odd = pair_rows(slope_ref[1], slope_ref[3])
+    newton = divisor * jnp.where(lanes % 2 == 0, even + pltpu.roll(even, width - 1, 1), odd + pltpu.roll(odd, 1, 1))
     newton_ref[...] = newton[:, :half]
     basis_slope = basis_slope_ref[...]
     lane = lanes[:1]
     same = jnp.sum(gram * basis_slope, axis=0, keepdims=True)
     turn = jnp.sum(swap_lanes(gram) * basis_slope, axis=0, keepdims=True)
     turn = jnp.where(lane % 2 == 0, turn, -turn)
-    fitted = jnp.where(lane % 2 == 0, same + swap_lanes(same), turn + swap_lanes(turn))
+    fitted = jnp.where(lane % 2 == 0, same + pltpu.roll(same, width - 1, 1), turn + pltpu.roll(turn, 1, 1))
     gradient_ref[...] = (-divisor * (sums - fitted))[:, :half]
 
 
@@ -498,25 +501,25 @@
     )(slab, modes_half, modes_other, w)
     total = pl.pallas_call(
         collect_kernel,
-        out_shape=jax.ShapeDtypeStruct((32, width), f32),
+        out_shape=jax.ShapeDtypeStruct(message.shape, f32),
         in_specs=[VMEM, ANY],
         out_specs=VMEM,
         compiler_params=PARAMS,
         name="collect",
     )(messages, done)
-    total = total + lax.ppermute(total, "tm", near)
-    total_in = lax.ppermute(total, "tm", wrap)
+    total_near = lax.ppermute(total, "tm", near)
+    total_far = lax.ppermute(jnp.concatenate([total, total_near]), "tm", wrap)
     gradient, gauss_newton = pl.pallas_call(
         lambda *refs: last_kernel(divisor, *refs),
         out_shape=(
             jax.ShapeDtypeStruct((1, basis), f32),
             jax.ShapeDtypeStruct((basis, basis), f32),
         ),
-        in_specs=[VMEM] * 4,
+        in_specs=[VMEM] * 5,
         out_specs=(VMEM, VMEM),
         compiler_params=PARAMS,
         name="newton",
-    )(total, total_in, slopes, basis_slope)
+    )(total, total_near, total_far, slopes, basis_slope)
     return spatial_modes, misfit, gradient.reshape(basis), gauss_newton
 
 

time: 49.8 us -> 49.5 us (level)
  no operation moved by 1% of the time
where the time goes in v4:
time: 49.5 us; the launch traced here: 49.4 us
  starting transfers between devices  23.5 us (47%)
  Pallas kernels  15.6 us (32%)
  waiting for transfers between devices  9.47 us (19%)
  between operations  0.72 us (1%)
    all_to_all x1, starting transfers between devices, local(): lax.all_to_all(messages, 'space', 0, 0, axis_index_groups=[list(range(spa...  11.8 us
    pallas_call x1, Pallas kernels, local(): pl.pallas_call(misfit_kernel, out_shape=(jax.ShapeDtypeStruct((basis, poi...  4.28 us
    ppermute x1, starting transfers between devices, local(): arrived = lax.ppermute(away, 'tm', flips(tm_size, 1))  3.33 us
    pallas_call x1, Pallas kernels, local(): pl.pallas_call(inverse_kernel, out_shape=jax.ShapeDtypeStruct((3 * width,...  2.89 us
    ppermute x1, starting transfers between devices, local(): total_far = lax.ppermute(jnp.concatenate([total, total_near]), 'tm', wrap)  2.68 us
    pallas_call x1, Pallas kernels, local(): pl.pallas_call(lambda *refs: first_kernel(complete, *refs), out_shape=(ja...  2.54 us
    pallas_call x1, Pallas kernels, local(): pl.pallas_call(lambda *refs: gram_kernel(complete, *refs), out_shape=(jax...  2.5 us
    ppermute x1, waiting for transfers between devices, local(): first_in = lax.ppermute(first, 'tm', wrap)  2.19 us
  transfers between devices with their start and end apart: 11, of which 8 were waited for; matrix products, arithmetic and copies ran while one was open for 0% of the time, Pallas kernels for 21%

profile of v4, /device:TPU:1, one launch (start us, length us, event | category | flops | bytes accessed | tf_op | source)
XLA Modules:
  0.0 49.4 jit_solution(6475843205943616667)
XLA Ops:
  0.6 0.0 copy-start
  0.6 2.5 %project_away.1 = (f32[512,128]{1,0:T(8,128)S(1)}, f32[512,128]{1,0:T(8,128)S(1)}, bf16[512,256]{1,0:T(8,128)(2,1)S(1)}, f32[1,32]{1,0:T(1,128)S(1)}, f32[1,32]{1,0:T(1,128)S(1)}) custom-call(f32[2048,512]{1,0:T(8,128)} %d_hbm.1, f32[1,32]{1,0:T(1,128)} %bitcast.3, f32[1,32]{1,0:T(1,128)} %bitcast.4), custom_call_target="tpu_custom_call" | custom-call | tf_op jit(solution)/shard_map/project_away/pallas_call | solution.py:404
  3.2 3.3 %collective-permute-start = (f32[512,128]{1,0:T(8,128)S(1)}, f32[512,128]{1,0:T(8,128)S(1)}, u32[]{:S(2)}, u32[]{:S(2)}) collective-permute-start(f32[512,128]{1,0:T(8,128)S(1)} %get-tuple-element.32), channel_id=1, source_target_pairs={{0,1},{1,0},{2,3},{3,2},{4,5},{5,4},{6,7},{7,6},{8,9},{9,8},{10,11... | collective-permute-start | bytes 786440 | tf_op jit(solution)/shard_map/ppermute | solution.py:419
  6.5 0.0 copy-done
  6.5 0.8 %project_kept.1 = (f32[256,128]{1,0:T(8,128)S(1)}, f32[256,128]{1,0:T(8,128)S(1)}, f32[512,128]{1,0:T(8,128)S(1)}) custom-call(f32[2048,512]{1,0:T(8,128)S(1)} %copy-done, bf16[512,256]{1,0:T(8,128)(2,1)S(1)} %get-tuple-element.30.w_ref), custom_call_target="tpu_custom_call" | custom-call | flops 536870912 | bytes 2097152 | tf_op jit(solution)/shard_map/project_kept/pallas_call | solution.py:421
  7.3 0.4 collective-permute-done
  7.7 0.1 collective-permute-start.1
  7.8 1.7 %collective-permute-start.3 = (f32[256,128]{1,0:T(8,128)S(1)}, f32[256,128]{1,0:T(8,128)S(1)}, u32[]{:S(2)}, u32[]{:S(2)}) collective-permute-start(f32[256,128]{1,0:T(8,128)S(1)} %get-tuple-element.42), channel_id=1, source_target_pairs={{0,7},{1,6},{2,5},{3,4},{4,3},{5,2},{6,1},{7,0},{8,15},{9,14},{10,... | collective-permute-start | bytes 393224 | tf_op jit(solution)/shard_map/ppermute | solution.py:436
  9.6 0.4 collective-permute-start.5
  9.9 2.5 %grams.1 = (f32[64,128]{1,0:T(8,128)S(1)}, f32[4,64,128]{2,1,0:T(8,128)S(1)}, f32[64,128]{1,0:T(8,128)S(1)}) custom-call(f32[1,32]{1,0:T(1,128)S(1)} %get-tuple-element.36.refs_0_, f32[1,32]{1,0:T(1,128)S(1)} %get-tuple-element.37.refs_1_, f32[512,128]{1,0:T(8,128)S(1)} %get-tuple-element.38.refs_2_.product_ref), custom_call_target="tpu_custom_call" | custom-call | flops 1000000000 | bytes 10000000 | tf_op jit(solution)/shard_map/grams/pallas_call | solution.py:437
  12.4 1.1 %collective-permute-done.1 = f32[256,128]{1,0:T(8,128)S(1)} collective-permute-done((f32[256,128]{1,0:T(8,128)S(1)}, f32[256,128]{1,0:T(8,128)S(1)}, u32[]{:S(2)}, u32[]{:S(2)}) %collective-permute-start.1) | collective-permute-done | bytes 131104 | tf_op jit(solution)/shard_map/ppermute | solution.py:435
  13.6 1.0 %collective-permute-start.2 = (f32[256,128]{1,0:T(8,128)S(1)}, f32[256,128]{1,0:T(8,128)S(1)}, u32[]{:S(2)}, u32[]{:S(2)}) collective-permute-start(f32[256,128]{1,0:T(8,128)S(1)} %add.14.first_ref), channel_id=1, source_target_pairs={{0,7},{1,6},{2,5},{3,4},{4,3},{5,2},{6,1},{7,0},{8,15},{9,14},{10,... | collective-permute-start | bytes 393224 | tf_op jit(solution)/shard_map/ppermute | solution.py:451
  14.7 0.0 collective-permute-done.3
  14.7 0.3 collective-permute-start.4
  15.0 2.9 %inverse.1.inverse_ref = bf16[384,256]{1,0:T(8,128)(2,1)S(1)} custom-call(f32[64,128]{1,0:T(8,128)S(1)} %get-tuple-element.44.gram_ref, f32[256,128]{1,0:T(8,128)S(1)} %add.15.after_ref.second_ref), custom_call_target="tpu_custom_call" | custom-call | flops 1000000000 | bytes 10000000 | tf_op jit(solution)/shard_map/inverse/pallas_call | solution.py:455
  17.9 2.2 %collective-permute-done.2.first_in_ref = f32[256,128]{1,0:T(8,128)S(1)} collective-permute-done((f32[256,128]{1,0:T(8,128)S(1)}, f32[256,128]{1,0:T(8,128)S(1)}, u32[]{:S(2)}, u32[]{:S(2)}) %collective-permute-start.2) | collective-permute-done | bytes 131104 | tf_op jit(solution)/shard_map/ppermute | solution.py:451
  20.1 0.3 collective-permute-done.4.second_in_ref
  20.4 0.0 collective-permute-done.5.product_in_ref
  20.4 1.0 %modes.1 = (f32[64,1024]{1,0:T(8,128)S(1)}, f32[8,128]{1,0:T(8,128)S(1)}) custom-call(f32[256,128]{1,0:T(8,128)S(1)} %add.14.first_ref, f32[256,128]{1,0:T(8,128)S(1)} %collective-permute-done.2.first_in_ref, f32[256,128]{1,0:T(8,128)S(1)} %add.15.after_ref.second_ref, f32[256,128]{1,0:T(8,128)S(1)} %collective-permute-done.4.second_in_ref, ...), custom_call_target="tpu_custom_call" | custom-call | tf_op jit(solution)/shard_map/modes/pallas_call | solution.py:464
  21.4 0.5 collective-permute-start.6
  21.9 0.1 collective-permute-start.7
  22.0 1.1 %collective-permute-done.7.b_ref = f32[8,128]{1,0:T(8,128)S(1)} collective-permute-done((f32[8,128]{1,0:T(8,128)S(1)}, f32[8,128]{1,0:T(8,128)S(1)}, u32[]{:S(2)}, u32[]{:S(2)}) %collective-permute-start.7) | collective-permute-done | bytes 4128 | tf_op jit(solution)/shard_map/ppermute | solution.py:476
  23.0 0.0 collective-permute-done.6.other_ref.after_ref
  23.0 0.7 %spread.1 = f32[32,8,128]{2,1,0:T(8,128)} custom-call(f32[8,128]{1,0:T(8,128)S(1)} %get-tuple-element.48.a_ref, f32[8,128]{1,0:T(8,128)S(1)} %collective-permute-done.7.b_ref, f32[64,1024]{1,0:T(8,128)S(1)} %collective-permute-done.6.other_ref.after_ref), custom_call_target="tpu_custom_call" | custom-call | tf_op jit(solution)/shard_map/spread/pallas_call | solution.py:478
  23.7 11.8 %all-to-all-start = ((f32[32,8,128]{2,1,0:T(8,128)}), f32[32,8,128]{2,1,0:T(8,128)S(1)}, u32[]{:S(2)}, u32[]{:S(2)}) async-start(f32[32,8,128]{2,1,0:T(8,128)} %spread.1), calls=%async_computation | async-start | bytes 262144 | tf_op jit(solution)/shard_map/all_to_all | solution.py:486
  35.5 4.3 %misfit.1 = (f32[64,2048]{1,0:T(8,128)}, f32[2048,512]{1,0:T(8,128)}, f32[8,128]{1,0:T(8,128)S(1)}) custom-call(f32[2048,512]{1,0:T(8,128)} %d_hbm.1, f32[64,1024]{1,0:T(8,128)S(1)} %get-tuple-element.45.own_ref, f32[64,1024]{1,0:T(8,128)S(1)} %collective-permute-done.6.other_ref.after_ref, bf16[512,256]{1,0:T(8,128)(2,1)S(1)} %get-tuple-element.30.w_ref), custom_call_target="tpu_custom_call" | custom-call | flops 1000000000 | bytes 10000000 | tf_op jit(solution)/shard_map/misfit/pallas_call | solution.py:488
  39.7 1.2 %all-to-all-done.messages_ref = f32[32,8,128]{2,1,0:T(8,128)S(1)} async-done(((f32[32,8,128]{2,1,0:T(8,128)}), f32[32,8,128]{2,1,0:T(8,128)S(1)}, u32[]{:S(2)}, u32[]{:S(2)}) %all-to-all-start) | async-done | bytes 131104 | tf_op jit(solution)/shard_map/all_to_all | solution.py:486
  41.0 1.5 %collective-permute-start.8 = (f32[8,128]{1,0:T(8,128)S(1)}, f32[8,128]{1,0:T(8,128)S(1)}, u32[]{:S(2)}, u32[]{:S(2)}) collective-permute-start(f32[8,128]{1,0:T(8,128)S(1)} %collect.1.refs_0_), channel_id=1, source_target_pairs={{0,3},{1,2},{2,1},{3,0},{4,7},{5,6},{6,5},{7,4},{8,11},{9,10},{10,... | collective-permute-start | bytes 12296 | tf_op jit(solution)/shard_map/ppermute | solution.py:510
  42.6 1.6 %collective-permute-done.8.refs_1_ = f32[8,128]{1,0:T(8,128)S(1)} collective-permute-done((f32[8,128]{1,0:T(8,128)S(1)}, f32[8,128]{1,0:T(8,128)S(1)}, u32[]{:S(2)}, u32[]{:S(2)}) %collective-permute-start.8) | collective-permute-done | bytes 4128 | tf_op jit(solution)/shard_map/ppermute | solution.py:510
  44.1 2.7 %collective-permute-start.9 = (f32[16,128]{1,0:T(8,128)S(1)}, f32[16,128]{1,0:T(8,128)S(1)}, u32[]{:S(2)}, u32[]{:S(2)}) collective-permute-start(f32[16,128]{1,0:T(8,128)S(1)} %pad_maximum_fusion), channel_id=1, source_target_pairs={{0,7},{1,6},{2,5},{3,4},{4,3},{5,2},{6,1},{7,0},{8,15},{9,14},{10,... | collective-permute-start | bytes 24584 | tf_op jit(solution)/shard_map/ppermute | solution.py:511
  46.8 1.6 %collective-permute-done.9.refs_2_ = f32[16,128]{1,0:T(8,128)S(1)} collective-permute-done((f32[16,128]{1,0:T(8,128)S(1)}, f32[16,128]{1,0:T(8,128)S(1)}, u32[]{:S(2)}, u32[]{:S(2)}) %collective-permute-start.9) | collective-permute-done | bytes 8224 | tf_op jit(solution)/shard_map/ppermute | solution.py:511
  48.4 0.9 %newton.1 = (f32[1,64]{1,0:T(1,128)}, f32[64,64]{1,0:T(8,128)}) custom-call(f32[8,128]{1,0:T(8,128)S(1)} %collect.1.refs_0_, f32[8,128]{1,0:T(8,128)S(1)} %collective-permute-done.8.refs_1_, f32[16,128]{1,0:T(8,128)S(1)} %collective-permute-done.9.refs_2_, f32[4,64,128]{2,1,0:T(8,128)S(1)} %get-tuple-element.50.refs_3_, f32[64,128]{1,0:T(8,128)S(1)} %get-tuple-element.51.refs_4_), custom_call_target="tpu_custom_call" | custom-call | tf_op jit(solution)/shard_map/newton/pallas_call | solution.py:512
  (5 shorter events, 0.1 us)
Async XLA Ops:
  0.6 5.9 %copy-start = (f32[2048,512]{1,0:T(8,128)S(1)}, f32[2048,512]{1,0:T(8,128)}, u32[]{:S(2)}) copy-start(f32[2048,512]{1,0:T(8,128)} %d_hbm.1) | copy-start | bytes 12582916
  3.2 4.5 %collective-permute-start = (f32[512,128]{1,0:T(8,128)S(1)}, f32[512,128]{1,0:T(8,128)S(1)}, u32[]{:S(2)}, u32[]{:S(2)}) collective-permute-start(f32[512,128]{1,0:T(8,128)S(1)} %get-tuple-element.32), channel_id=1, source_target_pairs={{0,1},{1,0},{2,3},{3,2},{4,5},{5,4},{6,7},{7,6},{8,9},{9,8},{10,11... | collective-permute-start | bytes 786440 | tf_op jit(solution)/shard_map/ppermute | solution.py:419
  7.7 5.9 %collective-permute-start.1 = (f32[256,128]{1,0:T(8,128)S(1)}, f32[256,128]{1,0:T(8,128)S(1)}, u32[]{:S(2)}, u32[]{:S(2)}) collective-permute-start(f32[256,128]{1,0:T(8,128)S(1)} %get-tuple-element.35), channel_id=1, source_target_pairs={{0,3},{1,2},{2,1},{3,0},{4,7},{5,6},{6,5},{7,4},{8,11},{9,10},{10,... | collective-permute-start | bytes 393224 | tf_op jit(solution)/shard_map/ppermute | solution.py:435
  7.8 6.8 %collective-permute-start.3 = (f32[256,128]{1,0:T(8,128)S(1)}, f32[256,128]{1,0:T(8,128)S(1)}, u32[]{:S(2)}, u32[]{:S(2)}) collective-permute-start(f32[256,128]{1,0:T(8,128)S(1)} %get-tuple-element.42), channel_id=1, source_target_pairs={{0,7},{1,6},{2,5},{3,4},{4,3},{5,2},{6,1},{7,0},{8,15},{9,14},{10,... | collective-permute-start | bytes 393224 | tf_op jit(solution)/shard_map/ppermute | solution.py:436
  9.6 10.8 %collective-permute-start.5 = (f32[512,128]{1,0:T(8,128)S(1)}, f32[512,128]{1,0:T(8,128)S(1)}, u32[]{:S(2)}, u32[]{:S(2)}) collective-permute-start(f32[512,128]{1,0:T(8,128)S(1)} %get-tuple-element.43), channel_id=1, source_target_pairs={{0,1},{1,0},{2,3},{3,2},{4,5},{5,4},{6,7},{7,6},{8,9},{9,8},{10,11... | collective-permute-start | bytes 786440 | tf_op jit(solution)/shard_map/ppermute | solution.py:434
  13.6 6.5 %collective-permute-start.2 = (f32[256,128]{1,0:T(8,128)S(1)}, f32[256,128]{1,0:T(8,128)S(1)}, u32[]{:S(2)}, u32[]{:S(2)}) collective-permute-start(f32[256,128]{1,0:T(8,128)S(1)} %add.14.first_ref), channel_id=1, source_target_pairs={{0,7},{1,6},{2,5},{3,4},{4,3},{5,2},{6,1},{7,0},{8,15},{9,14},{10,... | collective-permute-start | bytes 393224 | tf_op jit(solution)/shard_map/ppermute | solution.py:451
  14.7 5.7 %collective-permute-start.4 = (f32[256,128]{1,0:T(8,128)S(1)}, f32[256,128]{1,0:T(8,128)S(1)}, u32[]{:S(2)}, u32[]{:S(2)}) collective-permute-start(f32[256,128]{1,0:T(8,128)S(1)} %add.15.after_ref.second_ref), channel_id=1, source_target_pairs={{0,3},{1,2},{2,1},{3,0},{4,7},{5,6},{6,5},{7,4},{8,11},{9,10},{10,... | collective-permute-start | bytes 393224 | tf_op jit(solution)/shard_map/ppermute | solution.py:454
  21.4 1.7 %collective-permute-start.6 = (f32[64,1024]{1,0:T(8,128)S(1)}, f32[64,1024]{1,0:T(8,128)S(1)}, u32[]{:S(2)}, u32[]{:S(2)}) collective-permute-start(f32[64,1024]{1,0:T(8,128)S(1)} %get-tuple-element.45.own_ref), channel_id=1, source_target_pairs={{0,1},{1,0},{2,3},{3,2},{4,5},{5,4},{6,7},{7,6},{8,9},{9,8},{10,11... | collective-permute-start | bytes 786440 | tf_op jit(solution)/shard_map/ppermute | solution.py:477
  21.9 1.2 %collective-permute-start.7 = (f32[8,128]{1,0:T(8,128)S(1)}, f32[8,128]{1,0:T(8,128)S(1)}, u32[]{:S(2)}, u32[]{:S(2)}) collective-permute-start(f32[8,128]{1,0:T(8,128)S(1)} %get-tuple-element.48.a_ref), channel_id=1, source_target_pairs={{0,1},{1,0},{2,3},{3,2},{4,5},{5,4},{6,7},{7,6},{8,9},{9,8},{10,11... | collective-permute-start | bytes 12296 | tf_op jit(solution)/shard_map/ppermute | solution.py:476
  23.7 17.3 %all-to-all-start = ((f32[32,8,128]{2,1,0:T(8,128)}), f32[32,8,128]{2,1,0:T(8,128)S(1)}, u32[]{:S(2)}, u32[]{:S(2)}) async-start(f32[32,8,128]{2,1,0:T(8,128)} %spread.1), calls=%async_computation | async-start | bytes 262144 | tf_op jit(solution)/shard_map/all_to_all | solution.py:486
  41.0 3.1 %collective-permute-start.8 = (f32[8,128]{1,0:T(8,128)S(1)}, f32[8,128]{1,0:T(8,128)S(1)}, u32[]{:S(2)}, u32[]{:S(2)}) collective-permute-start(f32[8,128]{1,0:T(8,128)S(1)} %collect.1.refs_0_), channel_id=1, source_target_pairs={{0,3},{1,2},{2,1},{3,0},{4,7},{5,6},{6,5},{7,4},{8,11},{9,10},{10,... | collective-permute-start | bytes 12296 | tf_op jit(solution)/shard_map/ppermute | solution.py:510
  44.1 4.3 %collective-permute-start.9 = (f32[16,128]{1,0:T(8,128)S(1)}, f32[16,128]{1,0:T(8,128)S(1)}, u32[]{:S(2)}, u32[]{:S(2)}) collective-permute-start(f32[16,128]{1,0:T(8,128)S(1)} %pad_maximum_fusion), channel_id=1, source_target_pairs={{0,7},{1,6},{2,5},{3,4},{4,3},{5,2},{6,1},{7,0},{8,15},{9,14},{10,... | collective-permute-start | bytes 24584 | tf_op jit(solution)/shard_map/ppermute | solution.py:511
